TPU v7x, 32 devices: a whole 2x2x4 slice. The times are simulated.
32 devices in a mesh: expert: 8 (over z, x), dp: 4 (over y, core).
Axes of the slice: x: 2, y: 2, z: 4, core: 2. Of those that a mesh axis runs over, the one named last changes fastest.
Arguments:
- tokens: bfloat16 [1024, 3584], P('expert', 'dp'), may hold values from -6 to 6
- route_ids: int32 [1024, 8], P('expert'), may hold values from 0 to 7, as said below
- gate_scores: float32 [1024, 8], P('expert'), may hold values from 0.1 to 1, as said below
- up_weight: bfloat16 [8, 3584, 1024], P('expert', 'dp'), may hold values from -0.09375 to 0.09375
- down_weight: bfloat16 [8, 1024, 3584], P('expert', None, 'dp'), may hold values from -0.1875 to 0.1875
Outputs:
- mixed: bfloat16 [1024, 3584], P('expert', 'dp')
Inputs may be any that keep to these rules, and one draw needn't show every extreme that they name: `route_ids`: each row names 8 different experts. The same 2 experts are named by exactly 128 rows in every aligned block of 128 rows (the tokens of one device); in such a block every other expert is named by 128 - 1 or 128 rows. `gate_scores`: positive affinities.
All inputs are finite; a program needn't handle non-finite values.
Results may differ from a plain program's by a relative error of at most 0.017.
Values may be sent and summed in bfloat16 or wider, within the bound.
A program may use at most 64 MiB of HBM per device.

v0:
```python
import jax
import jax.numpy as jnp
from jax import lax
from jax.sharding import PartitionSpec as P

HOT = 2


ROUTE_SCALE = 2.5


def silu_hidden(before):
    summed = lax.psum(before.astype(jnp.bfloat16), "dp").astype(jnp.float32)
    result = jax.nn.silu(summed).astype(jnp.bfloat16)
    return result


def local(tokens, route_ids, gate_scores, up_weight, down_weight):
    token_count, chosen_count = route_ids.shape
    features = tokens.shape[1]
    experts = lax.axis_size("expert")
    mean_rows = token_count * chosen_count // experts
    hot_most = min(2 * mean_rows - 1, token_count)
    cold_rows = (experts - HOT) * mean_rows - HOT * (hot_most - mean_rows)
    cold_most = -(-cold_rows // (experts - HOT))
    flat_ids = route_ids.reshape(-1)
    row_total = flat_ids.shape[0]
    expert_range = jnp.arange(experts, dtype=jnp.int32)
    onehot = (flat_ids[:, None] == expert_range[None, :]).astype(jnp.int32)
    running = jnp.cumsum(onehot, axis=0) - 1
    row_ranks = jnp.sum(onehot * running, axis=1)
    padded = jnp.concatenate([tokens, jnp.zeros((1, features), tokens.dtype)], axis=0)
    up_local = up_weight[0]
    down_local = down_weight[0]
    mix_weights = gate_scores * (ROUTE_SCALE / jnp.sum(gate_scores, axis=1, keepdims=True))
    slot_count = max(hot_most, cold_most)
    slot_of_row = flat_ids * slot_count + row_ranks
    slot_table = jnp.full((experts * slot_count,), row_total, jnp.int32)
    slot_table = slot_table.at[slot_of_row].set(jnp.arange(row_total, dtype=jnp.int32), mode="drop")
    sending = padded[slot_table // chosen_count].reshape(experts, slot_count, features)
    arrived = lax.all_to_all(sending, "expert", split_axis=0, concat_axis=0, tiled=True)
    item_count = arrived.shape[1]
    flat_rows = arrived.reshape(-1, features)
    before = jnp.dot(flat_rows, up_local, preferred_element_type=jnp.float32)
    hidden = silu_hidden(before)
    output = jnp.dot(hidden, down_local, preferred_element_type=jnp.float32)
    outcome = output.astype(jnp.bfloat16).reshape(experts, item_count, features)
    returned = lax.all_to_all(outcome, "expert", split_axis=0, concat_axis=0, tiled=True).reshape(
        -1, features
    )
    picked = returned[slot_of_row]
    picked = picked.reshape(token_count, chosen_count, features).astype(jnp.float32)
    mixed = jnp.sum(mix_weights[:, :, None] * picked, axis=1)
    return mixed.astype(jnp.bfloat16)


def solution(mesh):
    return jax.shard_map(
        local,
        mesh=mesh,
        in_specs=(
            P("expert", "dp"),
            P("expert", None),
            P("expert", None),
            P("expert", "dp", None),
            P("expert", None, "dp"),
        ),
        out_specs=P("expert", "dp"),
        check_vma=False,
    )
```

profile of v0, /device:TPU:0, one launch (start us, length us, event | category | flops | bytes accessed | tf_op | source)
XLA Modules:
  0.0 197.8 jit_solution(4762432925685173164)
XLA Ops:
  6.5 0.0 copy-start
  6.5 0.9 copy.9
  7.5 0.1 eq.29
  7.6 0.1 eq.25
  7.6 0.7 broadcast_multiply_fusion
  8.3 2.3 %reduce-window.6 = s32[8,8,128]{2,1,0:T(8,128)S(1)} reduce-window(s32[8,8,128]{2,1,0:T(8,128)S(1)} %fusion.17, s32[]{:T(128)} %constant.32.clone.1), window={size=1x1x128 pad=0_0x0_0x127_0}, to_apply=%region_1.2 | reduce-window | flops 1040384 | bytes 65540 | tf_op jit(solution)/shard_map/reduce-window
  10.6 0.3 slice_reduce_fusion
  10.9 0.2 reduce-window.9
  11.0 0.1 add_bitcast_fusion
  11.1 0.1 copy.8
  11.2 0.1 mul.44
  11.4 4.3 %scatter_custom_fusion = s32[1024]{0:T(1024)S(1)} fusion(s32[1024]{0:T(1024)S(1)} %bitcast.37, s32[1024]{0:T(1024)S(1)} %iota.11, s32[]{:T(128)} %constant.30.clone.1), kind=kCustom, calls=%fused_computation.37 | custom fusion | bytes 4100 | tf_op jit(solution)/shard_map/scatter | solution.py:39
  15.7 1.0 concatenate.3
  16.7 5.3 %gather_fusion = bf16[1024,896]{1,0:T(8,128)(2,1)} fusion(bf16[129,896]{1,0:T(8,128)(2,1)S(1)} %concatenate.3, s32[1024]{0:T(1024)S(1)} %fusion.19), kind=kCustom, calls=%fused_computation | custom fusion | bytes 3674112 | tf_op jit(solution)/shard_map/gather | solution.py:40
  21.9 49.9 %all_to_all.10 = bf16[8,128,896]{2,1,0:T(8,128)(2,1)S(1)} all-to-all(bf16[8,128,896]{2,1,0:T(8,128)(2,1)} %bitcast.33), channel_id=1, replica_groups=mesh['expert'=8,'dp'=4] {'expert'}, dimensions={0} | all-to-all | bytes 3670016 | tf_op jit(solution)/shard_map/all_to_all | solution.py:41
  71.8 3.6 %convolution_convert_fusion = bf16[1024,1024]{1,0:T(8,128)(2,1)} fusion(bf16[1024,896]{1,0:T(8,128)(2,1)S(1)} %bitcast.35, bf16[1,896,1024]{2,1,0:T(8,128)(2,1)S(1)} %copy-done), kind=kOutput, calls=%fused_computation.13 | convolution fusion | flops 1880096768 | bytes 5767168 | tf_op jit(solution)/shard_map/dot_general | solution.py:44
  75.5 0.0 all-reduce.3.cloned.1.call-update
  75.5 50.6 %all-reduce.3.cloned.1.call-done = bf16[1024,1024]{1,0:T(8,128)(2,1)} async-done(((bf16[1024,1024]{1,0:T(8,128)(2,1)}), bf16[1024,1024]{1,0:T(8,128)(2,1)}) %all-reduce.3.cloned.1.call-update) | async-done | bytes 2097168 | tf_op jit(solution)/shard_map/psum | solution.py:13
  126.1 5.7 %fusion.10 = bf16[1024,896]{1,0:T(8,128)(2,1)} fusion(bf16[1,1024,896]{2,1,0:T(8,128)(2,1)} %param.9, bf16[1024,1024]{1,0:T(8,128)(2,1)} %all-reduce.3.cloned.1.call-done), kind=kOutput, calls=%fused_computation.16 | convolution fusion | flops 1886257152 | bytes 5767168 | tf_op jit(solution)/shard_map/dot_general | solution.py:46
  131.8 5.6 %all-to-all-start.1 = ((bf16[8,128,896]{2,1,0:T(8,128)(2,1)}), bf16[8,128,896]{2,1,0:T(8,128)(2,1)}, u32[]{:S(2)}, u32[]{:S(2)}) async-start(bf16[8,128,896]{2,1,0:T(8,128)(2,1)} %bitcast.34), calls=%async_computation.1 | async-start | bytes 3670016 | tf_op jit(solution)/shard_map/all_to_all | solution.py:48
  137.5 0.1 copy.7
  137.6 42.5 %all-to-all-done.1 = bf16[8,128,896]{2,1,0:T(8,128)(2,1)} async-done(((bf16[8,128,896]{2,1,0:T(8,128)(2,1)}), bf16[8,128,896]{2,1,0:T(8,128)(2,1)}, u32[]{:S(2)}, u32[]{:S(2)}) %all-to-all-start.1) | async-done | bytes 1835040 | tf_op jit(solution)/shard_map/all_to_all | solution.py:48
  180.1 7.5 %gather_fusion.1 = bf16[1024,896]{1,0:T(8,128)(2,1)} fusion(bf16[1024,896]{1,0:T(8,128)(2,1)} %bitcast.8, s32[1024]{0:T(1024)S(1)} %broadcast_clamp_fusion), kind=kCustom, calls=%fused_computation.1 | custom fusion | bytes 3674112 | tf_op jit(solution)/shard_map/gather | solution.py:51
  187.6 3.4 %fusion.4 = bf16[128,896]{1,0:T(8,128)(2,1)} fusion(bf16[1024,896]{1,0:T(8,128)(2,1)} %gather_fusion.1, f32[128,8]{1,0:T(8,128)S(1)} %copy.7), kind=kLoop, calls=%fused_computation.10 | loop fusion | flops 2637824 | bytes 2068480 | tf_op jit(solution)/shard_map/reduce_sum | solution.py:53
  (13 shorter events, 0.1 us)
Async XLA Ops:
  6.5 65.3 %copy-start = (bf16[1,896,1024]{2,1,0:T(8,128)(2,1)S(1)}, bf16[1,896,1024]{2,1,0:T(8,128)(2,1)}, u32[]{:S(2)}) copy-start(bf16[1,896,1024]{2,1,0:T(8,128)(2,1)} %param.8) | copy-start | bytes 5505028
  6.5 119.5 %all-reduce.3.cloned.1.call-start = ((), (), s32[]{:S(2)}) async-start(), calls=%async_computation.2 | async-start | bytes 4194304 | tf_op jit(solution)/shard_map/psum | solution.py:13
  131.8 5.6 %copy-start.1 = (f32[128,8]{0,1:T(8,128)S(1)}, f32[128,8]{0,1:T(8,128)}, u32[]{:S(2)}) copy-start(f32[128,8]{0,1:T(8,128)} %param.7) | copy-start | bytes 12292
  131.8 48.3 %all-to-all-start.1 = ((bf16[8,128,896]{2,1,0:T(8,128)(2,1)}), bf16[8,128,896]{2,1,0:T(8,128)(2,1)}, u32[]{:S(2)}, u32[]{:S(2)}) async-start(bf16[8,128,896]{2,1,0:T(8,128)(2,1)} %bitcast.34), calls=%async_computation.1 | async-start | bytes 3670016 | tf_op jit(solution)/shard_map/all_to_all | solution.py:48
Sparse Core Ops, SparseCore 0:
  75.6 50.4 all-reduce.2
where the time goes:
time: 198 us
  waiting for transfers between devices  93.1 us (47%)
  blocking collectives  49.9 us (25%)
  local copies, waits for them, and re-layouts  19.7 us (10%)
  between operations  13.5 us (7%)
  matrix products  9.39 us (5%)
  other arithmetic  6.64 us (3%)
  starting transfers between devices  5.65 us (3%)
    psum x1, waiting for transfers between devices, silu_hidden(): summed = lax.psum(before.astype(jnp.bfloat16), 'dp').astype(jnp.float32)  50.6 us
    all_to_all x1, blocking collectives, local(): lax.all_to_all(sending, 'expert', split_axis=0, concat_axis=0, tiled=True)  49.9 us
    all_to_all x1, waiting for transfers between devices, local(): lax.all_to_all(outcome, 'expert', split_axis=0, concat_axis=0, tiled=True)  42.5 us
    gather x1, local copies, waits for them, and re-layouts, local(): picked = returned[slot_of_row]  7.52 us
    dot_general x1, matrix products, local(): output = jnp.dot(hidden, down_local, preferred_element_type=jnp.float32)  5.74 us
    all_to_all x1, starting transfers between devices, local(): lax.all_to_all(outcome, 'expert', split_axis=0, concat_axis=0, tiled=True)  5.64 us
    gather x1, local copies, waits for them, and re-layouts, local(): padded[slot_table // chosen_count].reshape(experts, slot_count, features)  5.26 us
    scatter x1, local copies, waits for them, and re-layouts, local(): slot_table.at[slot_of_row]  4.31 us
  transfers between devices with their start and end apart: 2, of which 2 were waited for; matrix products, arithmetic and copies ran while one was open for 0% of the time, Pallas kernels for 0%

commit v1 on v0

--- a/solution.py
+++ b/solution.py
@@ -1,6 +1,10 @@
+import functools
+
 import jax
 import jax.numpy as jnp
 from jax import lax
+from jax.experimental import pallas as pl
+from jax.experimental.pallas import tpu as pltpu
 from jax.sharding import PartitionSpec as P
 
 HOT = 2
@@ -15,7 +19,7 @@
     return result
 
 
-def local(tokens, route_ids, gate_scores, up_weight, down_weight):
+def routed(tokens, route_ids, gate_scores, up_weight, down_weight):
     token_count, chosen_count = route_ids.shape
     features = tokens.shape[1]
     experts = lax.axis_size("expert")
@@ -54,6 +58,264 @@
     return mixed.astype(jnp.bfloat16)
 
 
+MESH = pl.DeviceIdType.MESH
+F32 = jnp.float32
+BF16 = jnp.bfloat16
+NZ, NX = 4, 2
+UNITS = NZ * NX
+
+
+def mesh_xor(z, d):
+    high = lax.rem(lax.div(z, 2) + lax.div(d, 2), 2)
+    low = lax.rem(lax.rem(z, 2) + lax.rem(d, 2), 2)
+    return high * 2 + low
+
+
+def dense_kernel(
+    tokens, route, gate, up, down, out,
+    got, upv, downv, wt, core_out, core_in, kept, y_out, y_in, hid, acc, x_out, x_in, z_out, z_in,
+    tok_s, tok_r, w_s, w_r, core_s, core_r, y_s, y_r, hid_s, hid_r, x_s, x_r, z_s, z_r, load,
+):
+    expert = lax.axis_index("expert")
+    part = lax.axis_index("dp")
+    z, x = lax.div(expert, NX), lax.rem(expert, NX)
+    y, core = lax.div(part, 2), lax.rem(part, 2)
+    half = upv.shape[2]
+    rows = tokens.shape[0]
+
+    def at(d, other):
+        xx = 1 - x if other else x
+        return {"expert": mesh_xor(z, d) * NX + xx}
+
+    x_peer = {"expert": z * NX + 1 - x}
+    core_peer = {"dp": y * 2 + 1 - core}
+    y_peer = {"dp": (1 - y) * 2 + core}
+
+    def remote(src, dst, send, recv, device):
+        return pltpu.make_async_remote_copy(
+            src_ref=src, dst_ref=dst, send_sem=send, recv_sem=recv,
+            device_id=device, device_id_type=MESH,
+        )
+
+    def tok_z(d):
+        return remote(tokens, got.at[2 * d], tok_s.at[2 * d], tok_r.at[2 * d], at(d, False))
+
+    def tok_x(d):
+        return remote(got.at[2 * d], got.at[2 * d + 1], tok_s.at[2 * d + 1], tok_r.at[2 * d + 1], x_peer)
+
+    def own_x():
+        return remote(tokens, got.at[1], tok_s.at[1], tok_r.at[1], x_peer)
+
+    def weight(k):
+        return remote(wt.at[0], wt.at[k], w_s.at[k], w_r.at[k], at(k // 2, k % 2 == 1))
+
+    def weight_in(u):
+        return remote(wt.at[0], wt.at[u], w_s.at[u], w_r.at[u], x_peer)
+
+    def core_copy(u):
+        return remote(core_out.at[u], core_in.at[u], core_s.at[u], core_r.at[u], core_peer)
+
+    def y_copy(u):
+        return remote(y_out.at[u], y_in.at[u], y_s.at[u], y_r.at[u], y_peer)
+
+    def hid_copy(u):
+        return remote(hid.at[u, 0], hid.at[u, 1], hid_s.at[u], hid_r.at[u], core_peer)
+
+    def x_copy(d):
+        return remote(x_out.at[d], x_in.at[d], x_s.at[d], x_r.at[d], x_peer)
+
+    def z_copy(d):
+        return remote(z_out.at[d], z_in.at[d], z_s.at[d], z_r.at[d], at(d, False))
+
+    own = pl.ds(pl.multiple_of(core * half, half), half)
+    theirs = pl.ds(pl.multiple_of((1 - core) * half, half), half)
+    loads = [
+        pltpu.make_async_copy(tokens, got.at[0], load.at[0]),
+        pltpu.make_async_copy(up.at[0, :, theirs], upv.at[1], load.at[1]),
+        pltpu.make_async_copy(up.at[0, :, own], upv.at[0], load.at[2]),
+        pltpu.make_async_copy(down.at[0, own, :], downv.at[0], load.at[3]),
+        pltpu.make_async_copy(down.at[0, theirs, :], downv.at[1], load.at[4]),
+    ]
+    for copy in loads:
+        copy.start()
+
+    barrier = pltpu.get_barrier_semaphore()
+    peers = [at(k // 2, k % 2 == 1) for k in range(1, UNITS)] + [core_peer, y_peer]
+    for peer in peers:
+        pl.semaphore_signal(barrier, inc=1, device_id=peer, device_id_type=MESH)
+    pl.semaphore_wait(barrier, len(peers))
+
+    own_x().start()
+    for d in range(1, NZ):
+        tok_z(d).start()
+
+    scores = gate[...]
+    mix = scores * (ROUTE_SCALE / jnp.sum(scores, axis=1, keepdims=True))
+    ids = route[...]
+    lanes = lax.broadcasted_iota(jnp.int32, (rows, 128), 1)
+    spread = jnp.zeros((rows, 128), F32)
+    for k in range(ids.shape[1]):
+        spread = spread + jnp.where(ids[:, k:k + 1] == lanes, mix[:, k:k + 1], 0.0)
+    wt[0] = spread.T[:UNITS, :]
+    for k in range(1, UNITS):
+        weight(k).start()
+    for copy in loads:
+        copy.wait()
+
+    def stage_a(u):
+        @pl.when(u >= 1)
+        def _():
+            remote(tokens, got.at[u], tok_s.at[u], tok_r.at[u], x_peer).wait_recv()
+
+        @pl.when((u >= 2) & (lax.rem(u, 2) == 0))
+        def _():
+            tok_x(lax.div(u, 2)).start()
+
+        block = got[u]
+        core_out[u] = jnp.dot(block, upv[1], preferred_element_type=F32).astype(BF16)
+        core_copy(u).start()
+        kept[u] = jnp.dot(block, upv[0], preferred_element_type=F32)
+
+    def stage_b(u):
+        core_copy(u).wait_recv()
+        total = kept[u] + core_in[u].astype(F32)
+        kept[u] = total
+        y_out[u] = total.astype(BF16)
+        y_copy(u).start()
+
+    def stage_c(u):
+        y_copy(u).wait_recv()
+        before = kept[u] + y_in[u].astype(F32)
+        hid[u, 0] = (before / (1.0 + jnp.exp(-before))).astype(BF16)
+        hid_copy(u).start()
+
+    def stage_d(u):
+        @pl.when(u >= 1)
+        def _():
+            weight_in(u).wait_recv()
+
+        scale = jnp.broadcast_to(wt[u, pl.ds(expert, 1), :], (128, rows)).T
+        hid_copy(u).wait_recv()
+        result = jnp.dot(hid[u, 0], downv[0], preferred_element_type=F32)
+        result = result + jnp.dot(hid[u, 1], downv[1], preferred_element_type=F32)
+        d = lax.div(u, 2)
+        result = result * jnp.concatenate([scale] * (result.shape[1] // 128), axis=1)
+
+        @pl.when(lax.rem(u, 2) == 0)
+        def _():
+            acc[d] = result
+
+        @pl.when(lax.rem(u, 2) == 1)
+        def _():
+            x_out[d] = result.astype(BF16)
+            x_copy(d).start()
+
+    def stage_e(d):
+        x_copy(d).wait_recv()
+        total = acc[d] + x_in[d].astype(F32)
+
+        @pl.when(d == 0)
+        def _():
+            acc[d] = total
+
+        @pl.when(d > 0)
+        def _():
+            z_out[d] = total.astype(BF16)
+            z_copy(d).start()
+
+    def step(t, carry):
+        @pl.when(t < UNITS)
+        def _():
+            stage_a(t)
+
+        @pl.when((t >= 1) & (t < UNITS + 1))
+        def _():
+            stage_b(t - 1)
+
+        @pl.when((t >= 2) & (t < UNITS + 2))
+        def _():
+            stage_c(t - 2)
+
+        @pl.when((t >= 3) & (t < UNITS + 3))
+        def _():
+            stage_d(t - 3)
+
+        @pl.when((t >= 5) & (lax.rem(t, 2) == 1))
+        def _():
+            stage_e(lax.div(t - 5, 2))
+
+        return carry
+
+    lax.fori_loop(0, UNITS + 4, step, 0)
+
+    total = acc[0]
+    for d in range(1, NZ):
+        z_copy(d).wait_recv()
+        total = total + z_in[d].astype(F32)
+    out[...] = total.astype(BF16)
+
+    own_x().wait_send()
+    for d in range(1, NZ):
+        tok_z(d).wait_send()
+        tok_x(d).wait_send()
+        z_copy(d).wait_send()
+    for d in range(NZ):
+        x_copy(d).wait_send()
+    for u in range(UNITS):
+        if u:
+            weight(u).wait_send()
+        core_copy(u).wait_send()
+        y_copy(u).wait_send()
+        hid_copy(u).wait_send()
+
+
+def dense(tokens, route_ids, gate_scores, up_weight, down_weight):
+    rows, features = tokens.shape
+    hidden = up_weight.shape[2]
+    half = hidden // 2
+    vmem = pl.BlockSpec(memory_space=pltpu.VMEM)
+    anywhere = pl.BlockSpec(memory_space=pl.ANY)
+    dma = pltpu.SemaphoreType.DMA
+    return pl.pallas_call(
+        dense_kernel,
+        out_shape=jax.ShapeDtypeStruct((rows, features), BF16),
+        in_specs=[anywhere, vmem, vmem, anywhere, anywhere],
+        out_specs=vmem,
+        scratch_shapes=[
+            pltpu.VMEM((UNITS, rows, features), BF16),
+            pltpu.VMEM((2, features, half), BF16),
+            pltpu.VMEM((2, half, features), BF16),
+            pltpu.VMEM((UNITS, UNITS, rows), F32),
+            pltpu.VMEM((UNITS, rows, half), BF16),
+            pltpu.VMEM((UNITS, rows, half), BF16),
+            pltpu.VMEM((UNITS, rows, half), F32),
+            pltpu.VMEM((UNITS, rows, half), BF16),
+            pltpu.VMEM((UNITS, rows, half), BF16),
+            pltpu.VMEM((UNITS, 2, rows, half), BF16),
+            pltpu.VMEM((NZ, rows, features), F32),
+            pltpu.VMEM((NZ, rows, features), BF16),
+            pltpu.VMEM((NZ, rows, features), BF16),
+            pltpu.VMEM((NZ, rows, features), BF16),
+            pltpu.VMEM((NZ, rows, features), BF16),
+        ] + [dma((UNITS,))] * 10 + [dma((NZ,))] * 4 + [dma((5,))],
+        compiler_params=pltpu.CompilerParams(
+            collective_id=0, has_side_effects=True, vmem_limit_bytes=40 * 2**20
+        ),
+        cost_estimate=pl.CostEstimate(
+            flops=4 * UNITS * rows * features * hidden,
+            bytes_accessed=4 * features * hidden + 4 * rows * features,
+            transcendentals=UNITS * rows * half,
+        ),
+    )(tokens, route_ids, gate_scores, up_weight, down_weight)
+
+
+def local(tokens, route_ids, gate_scores, up_weight, down_weight):
+    experts = lax.axis_size("expert")
+    every = route_ids.shape[1] == experts == UNITS and lax.axis_size("dp") == 4
+    body = dense if every and tokens.shape[0] == 128 else routed
+    return body(tokens, route_ids, gate_scores, up_weight, down_weight)
+
+
 def solution(mesh):
     return jax.shard_map(
         local,

time: 198 us -> 75.9 us (0.38)
  waiting for transfers between devices: 93.1 us -> 0 us
  Pallas kernels: 0 us -> 68.6 us
  blocking collectives: 49.9 us -> 0 us
  local copies, waits for them, and re-layouts: 19.7 us -> 6.19 us
  between operations: 13.5 us -> 0.02 us
  matrix products: 9.39 us -> 0 us
  other arithmetic: 6.64 us -> 0 us
  starting transfers between devices: 5.65 us -> 0 us
    pallas_call x0 -> x1, Pallas kernels: none -> 68.6 us  [dense(): pl.pallas_call(dense_kernel, out_shape=jax.ShapeDtypeStruct((rows, featur...]
    psum x1 -> x0, waiting for transfers between devices: 50.6 us -> none  [silu_hidden(): summed = lax.psum(before.astype(jnp.bfloat16), 'dp').astype(jnp.float32)]
    all_to_all x1 -> x0, blocking collectives: 49.9 us -> none  [local(): lax.all_to_all(sending, 'expert', split_axis=0, concat_axis=0, tiled=True)]
    all_to_all x1 -> x0, waiting for transfers between devices: 42.5 us -> none  [local(): lax.all_to_all(outcome, 'expert', split_axis=0, concat_axis=0, tiled=True)]
    gather x2 -> x0, local copies, waits for them, and re-layouts: 12.8 us -> none  [the longest x1 7.52 us: local(): picked = returned[slot_of_row]]
    dot_general x2 -> x0, matrix products: 9.39 us -> none  [the longest x1 5.74 us: local(): output = jnp.dot(hidden, down_local, preferred_element_type=jnp.float32)]
    all_to_all x1 -> x0, starting transfers between devices: 5.64 us -> none  [local(): lax.all_to_all(outcome, 'expert', split_axis=0, concat_axis=0, tiled=True)]
    unnamed x5 -> x9, local copies, waits for them, and re-layouts: 0.93 us -> 6.19 us
  transfers between devices with their start and end apart: 2 -> 0, of which waited for: 2 -> 0; matrix products, arithmetic and copies ran while one was open for 0% -> 0% of each run, Pallas kernels for 0% -> 0%
where the time goes in v1:
time: 75.9 us; the launch traced here: 74.8 us
  Pallas kernels  68.6 us (90%)
  local copies, waits for them, and re-layouts  6.19 us (8%)
    pallas_call x1, Pallas kernels, dense(): pl.pallas_call(dense_kernel, out_shape=jax.ShapeDtypeStruct((rows, featur...  68.6 us
    unnamed x9, local copies, waits for them, and re-layouts  6.19 us

profile of v1, /device:TPU:0, one launch (start us, length us, event | category | flops | bytes accessed | tf_op | source)
XLA Modules:
  0.0 74.8 jit_solution(16878889369852282954)
XLA Ops:
  0.0 0.8 %copy.6.route = s32[128,8]{1,0:T(8,128)S(1)} copy(s32[128,8]{0,1:T(8,128)} %param.6) | data formatting | bytes 8192 | tf_op args[1]
  0.8 0.8 %copy.7.gate = f32[128,8]{1,0:T(8,128)S(1)} copy(f32[128,8]{0,1:T(8,128)} %param.7) | data formatting | bytes 8192 | tf_op args[2]
  1.6 0.0 copy-start
  1.6 1.5 %copy-done = bf16[1,896,1024]{2,1,0:T(8,128)(2,1)S(1)} copy-done((bf16[1,896,1024]{2,1,0:T(8,128)(2,1)S(1)}, bf16[1,896,1024]{2,1,0:T(8,128)(2,1)}, u32[]{:S(2)}) %copy-start) | copy-done | bytes 1835032
  3.1 0.0 copy-start.1
  3.1 1.5 %copy-done.1 = bf16[1,1024,896]{2,1,0:T(8,128)(2,1)S(1)} copy-done((bf16[1,1024,896]{2,1,0:T(8,128)(2,1)S(1)}, bf16[1,1024,896]{2,1,0:T(8,128)(2,1)}, u32[]{:S(2)}) %copy-start.1) | copy-done | bytes 1835032
  4.6 0.0 copy-start.2
  4.6 0.9 %copy-done.2 = bf16[128,896]{1,0:T(8,128)(2,1)S(1)} copy-done((bf16[128,896]{1,0:T(8,128)(2,1)S(1)}, bf16[128,896]{1,0:T(8,128)(2,1)}, u32[]{:S(2)}) %copy-start.2) | copy-done | bytes 229400
  5.5 68.6 %shard_map.55 = bf16[128,896]{1,0:T(8,128)(2,1)S(1)} custom-call(bf16[128,896]{1,0:T(8,128)(2,1)S(1)} %copy-done.2, s32[128,8]{1,0:T(8,128)S(1)} %copy.6.route, f32[128,8]{1,0:T(8,128)S(1)} %copy.7.gate, bf16[1,896,1024]{2,1,0:T(8,128)(2,1)S(1)} %copy-done, bf16[1,1024,896]{2,1,0:T(8,128)(2,1)S(1)} %copy-done.1), custom_call_target="tpu_custom_call" | custom-call | flops 3758096384 | bytes 4128768 | tf_op jit(solution)/shard_map/pallas_call | solution.py:279
  74.1 0.7 copy.9
Async XLA Ops:
  1.6 1.5 %copy-start = (bf16[1,896,1024]{2,1,0:T(8,128)(2,1)S(1)}, bf16[1,896,1024]{2,1,0:T(8,128)(2,1)}, u32[]{:S(2)}) copy-start(bf16[1,896,1024]{2,1,0:T(8,128)(2,1)} %up.1) | copy-start | bytes 5505028
  3.1 1.5 %copy-start.1 = (bf16[1,1024,896]{2,1,0:T(8,128)(2,1)S(1)}, bf16[1,1024,896]{2,1,0:T(8,128)(2,1)}, u32[]{:S(2)}) copy-start(bf16[1,1024,896]{2,1,0:T(8,128)(2,1)} %down.1) | copy-start | bytes 5505028
  4.6 0.9 %copy-start.2 = (bf16[128,896]{1,0:T(8,128)(2,1)S(1)}, bf16[128,896]{1,0:T(8,128)(2,1)}, u32[]{:S(2)}) copy-start(bf16[128,896]{1,0:T(8,128)(2,1)} %tokens.1) | copy-start | bytes 688132

commit v2 on v1

--- a/solution.py
+++ b/solution.py
@@ -73,7 +73,7 @@
 
 def dense_kernel(
     tokens, route, gate, up, down, out,
-    got, upv, downv, wt, core_out, core_in, kept, y_out, y_in, hid, acc, x_out, x_in, z_out, z_in,
+    got, upv, downv, wt, core_out, core_in, kept, y_out, y_in, hid, acc, over, x_out, x_in, z_out, z_in,
     tok_s, tok_r, w_s, w_r, core_s, core_r, y_s, y_r, hid_s, hid_r, x_s, x_r, z_s, z_r, load,
 ):
     expert = lax.axis_index("expert")
@@ -97,14 +97,25 @@
             device_id=device, device_id_type=MESH,
         )
 
-    def tok_z(d):
-        return remote(tokens, got.at[2 * d], tok_s.at[2 * d], tok_r.at[2 * d], at(d, False))
-
-    def tok_x(d):
-        return remote(got.at[2 * d], got.at[2 * d + 1], tok_s.at[2 * d + 1], tok_r.at[2 * d + 1], x_peer)
-
-    def own_x():
-        return remote(tokens, got.at[1], tok_s.at[1], tok_r.at[1], x_peer)
+    inner = lax.rem(mesh_xor(z, lax.div(z, 2)), 2)
+    is_inner = inner == 1
+    near, across = at(1, False), at(3, False)
+
+    def token(k, src, slot, device):
+        return remote(src, got.at[slot], tok_s.at[k], tok_r.at[slot], device)
+
+    def token_in(u):
+        return remote(tokens, got.at[u], tok_s.at[0], tok_r.at[u], x_peer)
+
+    own_x = token(0, tokens, 1, x_peer)
+    own_near = token(1, tokens, 2, near)
+    own_across = token(2, tokens, 6, across)
+    near_across = token(3, got.at[2], 4, across)
+    side_near = token(4, got.at[1], 3, near)
+    across_near = token(5, got.at[6], 4, near)
+    far_near = token(6, got.at[4], 6, near)
+    middle_x = token(7, got.at[4], 5, x_peer)
+    last_x = token(8, got.at[6], 7, x_peer)
 
     def weight(k):
         return remote(wt.at[0], wt.at[k], w_s.at[k], w_r.at[k], at(k // 2, k % 2 == 1))
@@ -123,6 +134,9 @@
 
     def x_copy(d):
         return remote(x_out.at[d], x_in.at[d], x_s.at[d], x_r.at[d], x_peer)
+
+    def over_copy():
+        return remote(over.at[1], over.at[2], z_s.at[0], z_r.at[0], near)
 
     def z_copy(d):
         return remote(z_out.at[d], z_in.at[d], z_s.at[d], z_r.at[d], at(d, False))
@@ -145,31 +159,54 @@
         pl.semaphore_signal(barrier, inc=1, device_id=peer, device_id_type=MESH)
     pl.semaphore_wait(barrier, len(peers))
 
-    own_x().start()
-    for d in range(1, NZ):
-        tok_z(d).start()
+    own_x.start()
+    own_near.start()
+
+    @pl.when(is_inner)
+    def _():
+        own_across.start()
 
     scores = gate[...]
-    mix = scores * (ROUTE_SCALE / jnp.sum(scores, axis=1, keepdims=True))
+    mix = scores * (ROUTE_SCALE / jnp.sum(scores, axis=0, keepdims=True))
     ids = route[...]
-    lanes = lax.broadcasted_iota(jnp.int32, (rows, 128), 1)
-    spread = jnp.zeros((rows, 128), F32)
-    for k in range(ids.shape[1]):
-        spread = spread + jnp.where(ids[:, k:k + 1] == lanes, mix[:, k:k + 1], 0.0)
-    wt[0] = spread.T[:UNITS, :]
+    named = lax.broadcasted_iota(jnp.int32, (UNITS, rows), 0)
+    spread = jnp.zeros((UNITS, rows), F32)
+    for k in range(UNITS):
+        spread = spread + jnp.where(ids[k:k + 1, :] == named, mix[k:k + 1, :], 0.0)
+    wt[0] = spread
     for k in range(1, UNITS):
         weight(k).start()
     for copy in loads:
         copy.wait()
 
     def stage_a(u):
-        @pl.when(u >= 1)
-        def _():
-            remote(tokens, got.at[u], tok_s.at[u], tok_r.at[u], x_peer).wait_recv()
-
-        @pl.when((u >= 2) & (lax.rem(u, 2) == 0))
-        def _():
-            tok_x(lax.div(u, 2)).start()
+        @pl.when(u > 0)
+        def _():
+            token_in(u).wait_recv()
+
+        @pl.when(u == 1)
+        def _():
+            side_near.start()
+
+        @pl.when((u == 2) & is_inner)
+        def _():
+            near_across.start()
+
+        @pl.when(u == 4)
+        def _():
+            middle_x.start()
+
+        @pl.when(u == 6)
+        def _():
+            last_x.start()
+
+        @pl.when((u == 4) & is_inner)
+        def _():
+            far_near.start()
+
+        @pl.when((u == 6) & is_inner)
+        def _():
+            across_near.start()
 
         block = got[u]
         core_out[u] = jnp.dot(block, upv[1], preferred_element_type=F32).astype(BF16)
@@ -201,66 +238,91 @@
         d = lax.div(u, 2)
         result = result * jnp.concatenate([scale] * (result.shape[1] // 128), axis=1)
 
-        @pl.when(lax.rem(u, 2) == 0)
+        @pl.when((lax.rem(u, 2) == 0) & (u != 2))
         def _():
             acc[d] = result
 
-        @pl.when(lax.rem(u, 2) == 1)
+        @pl.when(u == 2)
+        def _():
+            z_out[1] = result.astype(BF16)
+            z_copy(1).start()
+
+        @pl.when(u == 1)
+        def _():
+            over[0] = result.astype(BF16)
+
+        @pl.when(u == 3)
+        def _():
+            over[1] = result.astype(BF16)
+            over_copy().start()
+
+        @pl.when((u == 5) | (u == 7))
         def _():
             x_out[d] = result.astype(BF16)
             x_copy(d).start()
 
     def stage_e(d):
         x_copy(d).wait_recv()
-        total = acc[d] + x_in[d].astype(F32)
-
-        @pl.when(d == 0)
-        def _():
-            acc[d] = total
-
-        @pl.when(d > 0)
-        def _():
-            z_out[d] = total.astype(BF16)
-            z_copy(d).start()
+        z_out[d] = (acc[d] + x_in[d].astype(F32)).astype(BF16)
+        z_copy(d).start()
+
+    outer_order, inner_order = [0, 2, 1, 4, 5, 6, 3, 7], [0, 2, 1, 6, 7, 4, 3, 5]
+    packed = [sum(v << (3 * k) for k, v in enumerate(o)) for o in (outer_order, inner_order)]
+    order = packed[0] + inner * (packed[1] - packed[0])
+
+    def slot(k):
+        return lax.rem(lax.shift_right_logical(order, 3 * k), UNITS)
 
     def step(t, carry):
         @pl.when(t < UNITS)
         def _():
-            stage_a(t)
+            stage_a(slot(t))
 
         @pl.when((t >= 1) & (t < UNITS + 1))
         def _():
-            stage_b(t - 1)
+            stage_b(slot(t - 1))
 
         @pl.when((t >= 2) & (t < UNITS + 2))
         def _():
-            stage_c(t - 2)
+            stage_c(slot(t - 2))
 
         @pl.when((t >= 3) & (t < UNITS + 3))
         def _():
-            stage_d(t - 3)
-
-        @pl.when((t >= 5) & (lax.rem(t, 2) == 1))
-        def _():
-            stage_e(lax.div(t - 5, 2))
+            stage_d(slot(t - 3))
+
+        @pl.when(t == 9)
+        def _():
+            stage_e(lax.div(slot(3), 2))
 
         return carry
 
-    lax.fori_loop(0, UNITS + 4, step, 0)
-
-    total = acc[0]
+    lax.fori_loop(0, UNITS + 3, step, 0)
+
+    over_copy().wait_recv()
+    x_out[0] = (over[0].astype(F32) + over[2].astype(F32)).astype(BF16)
+    x_copy(0).start()
+    stage_e(lax.div(slot(7), 2))
+
+    x_copy(0).wait_recv()
+    total = acc[0] + x_in[0].astype(F32)
     for d in range(1, NZ):
         z_copy(d).wait_recv()
         total = total + z_in[d].astype(F32)
     out[...] = total.astype(BF16)
 
-    own_x().wait_send()
-    for d in range(1, NZ):
-        tok_z(d).wait_send()
-        tok_x(d).wait_send()
-        z_copy(d).wait_send()
+    for copy in (own_x, own_near, side_near, middle_x, last_x, over_copy()):
+        copy.wait_send()
+
+    @pl.when(is_inner)
+    def _():
+        for copy in (own_across, near_across, far_near, across_near):
+            copy.wait_send()
+
     for d in range(NZ):
-        x_copy(d).wait_send()
+        if d:
+            z_copy(d).wait_send()
+        if d != 1:
+            x_copy(d).wait_send()
     for u in range(UNITS):
         if u:
             weight(u).wait_send()
@@ -293,20 +355,21 @@
             pltpu.VMEM((UNITS, rows, half), BF16),
             pltpu.VMEM((UNITS, 2, rows, half), BF16),
             pltpu.VMEM((NZ, rows, features), F32),
+            pltpu.VMEM((3, rows, features), BF16),
             pltpu.VMEM((NZ, rows, features), BF16),
             pltpu.VMEM((NZ, rows, features), BF16),
             pltpu.VMEM((NZ, rows, features), BF16),
             pltpu.VMEM((NZ, rows, features), BF16),
-        ] + [dma((UNITS,))] * 10 + [dma((NZ,))] * 4 + [dma((5,))],
+        ] + [dma((9,))] + [dma((UNITS,))] * 9 + [dma((NZ,))] * 4 + [dma((5,))],
         compiler_params=pltpu.CompilerParams(
-            collective_id=0, has_side_effects=True, vmem_limit_bytes=40 * 2**20
+            collective_id=0, has_side_effects=True, vmem_limit_bytes=63 * 2**20
         ),
         cost_estimate=pl.CostEstimate(
             flops=4 * UNITS * rows * features * hidden,
             bytes_accessed=4 * features * hidden + 4 * rows * features,
             transcendentals=UNITS * rows * half,
         ),
-    )(tokens, route_ids, gate_scores, up_weight, down_weight)
+    )(tokens, route_ids.T, gate_scores.T, up_weight, down_weight)
 
 
 def local(tokens, route_ids, gate_scores, up_weight, down_weight):

time: 75.9 us -> 74.3 us (0.979); the launches traced: 74.8 us -> 74.1 us
  local copies, waits for them, and re-layouts: 6.19 us -> 1.65 us
  Pallas kernels: 68.6 us -> 72.5 us
    unnamed x9 -> x1, local copies, waits for them, and re-layouts: 6.19 us -> 1.65 us
    pallas_call x1, Pallas kernels: 68.6 us -> 72.5 us  [dense(): pl.pallas_call(dense_kernel, out_shape=jax.ShapeDtypeStruct((rows, featur...]
where the time goes in v2:
time: 74.3 us; the launch traced here: 74.1 us
  Pallas kernels  72.5 us (98%)
  local copies, waits for them, and re-layouts  1.65 us (2%)
    pallas_call x1, Pallas kernels, dense(): pl.pallas_call(dense_kernel, out_shape=jax.ShapeDtypeStruct((rows, featur...  72.5 us
    unnamed x1, local copies, waits for them, and re-layouts  1.65 us

profile of v2, /device:TPU:0, one launch (start us, length us, event | category | flops | bytes accessed | tf_op | source)
XLA Modules:
  0.0 74.1 jit_solution(7641193858256012276)
XLA Ops:
  0.0 72.5 %shard_map.55 = bf16[128,896]{1,0:T(8,128)(2,1)} custom-call(bf16[128,896]{1,0:T(8,128)(2,1)} %tokens.1, s32[8,128]{1,0:T(8,128)} %bitcast.2, f32[8,128]{1,0:T(8,128)} %bitcast.3, bf16[1,896,1024]{2,1,0:T(8,128)(2,1)} %up.1, bf16[1,1024,896]{2,1,0:T(8,128)(2,1)} %down.1), custom_call_target="tpu_custom_call" | custom-call | flops 3758096384 | bytes 4128768 | tf_op jit(solution)/shard_map/pallas_call | solution.py:341
  72.5 1.6 %copy.7 = bf16[128,896]{1,0:T(8,128)(2,1)} copy(bf16[128,896]{1,0:T(8,128)(2,1)} %shard_map.55) | data formatting | bytes 458752

commit v3 on v2

--- a/solution.py
+++ b/solution.py
@@ -107,15 +107,16 @@
     def token_in(u):
         return remote(tokens, got.at[u], tok_s.at[0], tok_r.at[u], x_peer)
 
-    own_x = token(0, tokens, 1, x_peer)
-    own_near = token(1, tokens, 2, near)
-    own_across = token(2, tokens, 6, across)
-    near_across = token(3, got.at[2], 4, across)
-    side_near = token(4, got.at[1], 3, near)
-    across_near = token(5, got.at[6], 4, near)
-    far_near = token(6, got.at[4], 6, near)
-    middle_x = token(7, got.at[4], 5, x_peer)
-    last_x = token(8, got.at[6], 7, x_peer)
+    second, third = 2 + inner, 3 - inner
+    own_x = token(0, tokens, 2, x_peer)
+    own_near = token(1, tokens, 1, near)
+    own_across = token(2, tokens, 3, across)
+    near_across = token(3, got.at[1], 5, across)
+    side_near = token(4, got.at[2], 6, near)
+    across_near = token(5, got.at[3], 3, near)
+    far_near = token(6, got.at[5], 5, near)
+    second_x = token(7, got.at[3], 4, x_peer)
+    third_x = token(8, got.at[5], 7, x_peer)
 
     def weight(k):
         return remote(wt.at[0], wt.at[k], w_s.at[k], w_r.at[k], at(k // 2, k % 2 == 1))
@@ -179,34 +180,47 @@
     for copy in loads:
         copy.wait()
 
+    def first_arrivals():
+        token_in(1).wait_recv()
+
+        @pl.when(is_inner)
+        def _():
+            near_across.start()
+            token_in(3).wait_recv()
+            across_near.start()
+            second_x.start()
+
+        token_in(2).wait_recv()
+
+        @pl.when(jnp.logical_not(is_inner))
+        def _():
+            side_near.start()
+
+    def second_arrivals():
+        @pl.when(is_inner)
+        def _():
+            token_in(5).wait_recv()
+            far_near.start()
+            side_near.start()
+            third_x.start()
+
+        @pl.when(jnp.logical_not(is_inner))
+        def _():
+            token_in(3).wait_recv()
+            second_x.start()
+
+    def third_arrivals():
+        @pl.when(jnp.logical_not(is_inner))
+        def _():
+            token_in(5).wait_recv()
+            third_x.start()
+
+        token_in(4).wait_recv()
+
     def stage_a(u):
-        @pl.when(u > 0)
+        @pl.when(u >= 6)
         def _():
             token_in(u).wait_recv()
-
-        @pl.when(u == 1)
-        def _():
-            side_near.start()
-
-        @pl.when((u == 2) & is_inner)
-        def _():
-            near_across.start()
-
-        @pl.when(u == 4)
-        def _():
-            middle_x.start()
-
-        @pl.when(u == 6)
-        def _():
-            last_x.start()
-
-        @pl.when((u == 4) & is_inner)
-        def _():
-            far_near.start()
-
-        @pl.when((u == 6) & is_inner)
-        def _():
-            across_near.start()
 
         block = got[u]
         core_out[u] = jnp.dot(block, upv[1], preferred_element_type=F32).astype(BF16)
@@ -227,36 +241,40 @@
         hid_copy(u).start()
 
     def stage_d(u):
+        other = (u == 2) | (u == 4) | (u >= 6)
+        d = jnp.where((u == 1) | (u == 6), 1, jnp.where((u == 3) | (u == 4), second, third))
+        d = jnp.where((u == 0) | (u == 2), 0, d)
+        k = 2 * d + other.astype(jnp.int32)
+
         @pl.when(u >= 1)
         def _():
-            weight_in(u).wait_recv()
-
-        scale = jnp.broadcast_to(wt[u, pl.ds(expert, 1), :], (128, rows)).T
+            weight_in(k).wait_recv()
+
+        scale = jnp.broadcast_to(wt[k, pl.ds(expert, 1), :], (128, rows)).T
         hid_copy(u).wait_recv()
         result = jnp.dot(hid[u, 0], downv[0], preferred_element_type=F32)
         result = result + jnp.dot(hid[u, 1], downv[1], preferred_element_type=F32)
-        d = lax.div(u, 2)
         result = result * jnp.concatenate([scale] * (result.shape[1] // 128), axis=1)
 
-        @pl.when((lax.rem(u, 2) == 0) & (u != 2))
+        @pl.when((u == 0) | (u == 3) | (u == 5))
         def _():
             acc[d] = result
 
-        @pl.when(u == 2)
+        @pl.when(u == 1)
         def _():
             z_out[1] = result.astype(BF16)
             z_copy(1).start()
 
-        @pl.when(u == 1)
+        @pl.when(u == 2)
         def _():
             over[0] = result.astype(BF16)
 
-        @pl.when(u == 3)
+        @pl.when(u == 6)
         def _():
             over[1] = result.astype(BF16)
             over_copy().start()
 
-        @pl.when((u == 5) | (u == 7))
+        @pl.when((u == 4) | (u == 7))
         def _():
             x_out[d] = result.astype(BF16)
             x_copy(d).start()
@@ -266,42 +284,47 @@
         z_out[d] = (acc[d] + x_in[d].astype(F32)).astype(BF16)
         z_copy(d).start()
 
-    outer_order, inner_order = [0, 2, 1, 4, 5, 6, 3, 7], [0, 2, 1, 6, 7, 4, 3, 5]
-    packed = [sum(v << (3 * k) for k, v in enumerate(o)) for o in (outer_order, inner_order)]
-    order = packed[0] + inner * (packed[1] - packed[0])
-
-    def slot(k):
-        return lax.rem(lax.shift_right_logical(order, 3 * k), UNITS)
-
     def step(t, carry):
+        @pl.when(t == 1)
+        def _():
+            first_arrivals()
+
+        @pl.when(t == 3)
+        def _():
+            second_arrivals()
+
+        @pl.when(t == 4)
+        def _():
+            third_arrivals()
+
         @pl.when(t < UNITS)
         def _():
-            stage_a(slot(t))
+            stage_a(t)
 
         @pl.when((t >= 1) & (t < UNITS + 1))
         def _():
-            stage_b(slot(t - 1))
+            stage_b(t - 1)
 
         @pl.when((t >= 2) & (t < UNITS + 2))
         def _():
-            stage_c(slot(t - 2))
+            stage_c(t - 2)
 
         @pl.when((t >= 3) & (t < UNITS + 3))
         def _():
-            stage_d(slot(t - 3))
-
-        @pl.when(t == 9)
-        def _():
-            stage_e(lax.div(slot(3), 2))
+            stage_d(t - 3)
+
+        @pl.when(t == 8)
+        def _():
+            stage_e(second)
 
         return carry
 
     lax.fori_loop(0, UNITS + 3, step, 0)
 
+    stage_e(third)
     over_copy().wait_recv()
     x_out[0] = (over[0].astype(F32) + over[2].astype(F32)).astype(BF16)
     x_copy(0).start()
-    stage_e(lax.div(slot(7), 2))
 
     x_copy(0).wait_recv()
     total = acc[0] + x_in[0].astype(F32)
@@ -310,7 +333,7 @@
         total = total + z_in[d].astype(F32)
     out[...] = total.astype(BF16)
 
-    for copy in (own_x, own_near, side_near, middle_x, last_x, over_copy()):
+    for copy in (own_x, own_near, side_near, second_x, third_x, over_copy()):
         copy.wait_send()
 
     @pl.when(is_inner)
@@ -336,12 +359,12 @@
     hidden = up_weight.shape[2]
     half = hidden // 2
     vmem = pl.BlockSpec(memory_space=pltpu.VMEM)
-    anywhere = pl.BlockSpec(memory_space=pl.ANY)
+    hbm = pl.BlockSpec(memory_space=pltpu.HBM)
     dma = pltpu.SemaphoreType.DMA
     return pl.pallas_call(
         dense_kernel,
         out_shape=jax.ShapeDtypeStruct((rows, features), BF16),
-        in_specs=[anywhere, vmem, vmem, anywhere, anywhere],
+        in_specs=[hbm, vmem, vmem, hbm, hbm],
         out_specs=vmem,
         scratch_shapes=[
             pltpu.VMEM((UNITS, rows, features), BF16),

time: 74.3 us -> 65.3 us (0.88)
  Pallas kernels: 72.5 us -> 63.4 us
    pallas_call x1, Pallas kernels: 72.5 us -> 63.4 us  [dense(): pl.pallas_call(dense_kernel, out_shape=jax.ShapeDtypeStruct((rows, featur...]
where the time goes in v3:
time: 65.3 us; the launch traced here: 65.1 us
  Pallas kernels  63.4 us (97%)
  local copies, waits for them, and re-layouts  1.65 us (3%)
    pallas_call x1, Pallas kernels, dense(): pl.pallas_call(dense_kernel, out_shape=jax.ShapeDtypeStruct((rows, featur...  63.4 us
    unnamed x1, local copies, waits for them, and re-layouts  1.65 us

profile of v3, /device:TPU:0, one launch (start us, length us, event | category | flops | bytes accessed | tf_op | source)
XLA Modules:
  0.0 65.1 jit_solution(1166604536579123174)
XLA Ops:
  0.0 63.4 %shard_map.55 = bf16[128,896]{1,0:T(8,128)(2,1)} custom-call(bf16[128,896]{1,0:T(8,128)(2,1)} %tokens.1, s32[8,128]{1,0:T(8,128)} %bitcast.2, f32[8,128]{1,0:T(8,128)} %bitcast.3, bf16[1,896,1024]{2,1,0:T(8,128)(2,1)} %up.1, bf16[1,1024,896]{2,1,0:T(8,128)(2,1)} %down.1), custom_call_target="tpu_custom_call" | custom-call | flops 3758096384 | bytes 4128768 | tf_op jit(solution)/shard_map/pallas_call | solution.py:364
  63.5 1.6 %copy.7 = bf16[128,896]{1,0:T(8,128)(2,1)} copy(bf16[128,896]{1,0:T(8,128)(2,1)} %shard_map.55) | data formatting | bytes 458752

commit v4 on v3

--- a/solution.py
+++ b/solution.py
@@ -101,11 +101,17 @@
     is_inner = inner == 1
     near, across = at(1, False), at(3, False)
 
+    part_rows = rows // 2
+
     def token(k, src, slot, device):
-        return remote(src, got.at[slot], tok_s.at[k], tok_r.at[slot], device)
-
-    def token_in(u):
-        return remote(tokens, got.at[u], tok_s.at[0], tok_r.at[u], x_peer)
+        def piece(p):
+            lines = pl.ds(p * part_rows, part_rows)
+            return remote(src.at[lines], got.at[slot, lines], tok_s.at[k, p], tok_r.at[slot, p], device)
+        return piece
+
+    def token_in(u, p):
+        lines = pl.ds(p * part_rows, part_rows)
+        return remote(tokens.at[lines], got.at[u, lines], tok_s.at[0, p], tok_r.at[u, p], x_peer)
 
     second, third = 2 + inner, 3 - inner
     own_x = token(0, tokens, 2, x_peer)
@@ -160,12 +166,19 @@
         pl.semaphore_signal(barrier, inc=1, device_id=peer, device_id_type=MESH)
     pl.semaphore_wait(barrier, len(peers))
 
-    own_x.start()
-    own_near.start()
+    own_x(0).start()
+    own_near(0).start()
 
     @pl.when(is_inner)
     def _():
-        own_across.start()
+        own_across(0).start()
+
+    own_x(1).start()
+    own_near(1).start()
+
+    @pl.when(is_inner)
+    def _():
+        own_across(1).start()
 
     scores = gate[...]
     mix = scores * (ROUTE_SCALE / jnp.sum(scores, axis=0, keepdims=True))
@@ -181,46 +194,55 @@
         copy.wait()
 
     def first_arrivals():
-        token_in(1).wait_recv()
+        for p in range(2):
+            token_in(1, p).wait_recv()
+
+            @pl.when(is_inner)
+            def _():
+                near_across(p).start()
+                token_in(3, p).wait_recv()
+                across_near(p).start()
+                second_x(p).start()
+
+            token_in(2, p).wait_recv()
+
+            @pl.when(jnp.logical_not(is_inner))
+            def _():
+                side_near(p).start()
+
+    def second_arrivals():
+        for p in range(2):
+            @pl.when(is_inner)
+            def _():
+                token_in(5, p).wait_recv()
+                far_near(p).start()
+                third_x(p).start()
+
+            @pl.when(jnp.logical_not(is_inner))
+            def _():
+                token_in(3, p).wait_recv()
+                second_x(p).start()
 
         @pl.when(is_inner)
         def _():
-            near_across.start()
-            token_in(3).wait_recv()
-            across_near.start()
-            second_x.start()
-
-        token_in(2).wait_recv()
-
-        @pl.when(jnp.logical_not(is_inner))
-        def _():
-            side_near.start()
-
-    def second_arrivals():
-        @pl.when(is_inner)
-        def _():
-            token_in(5).wait_recv()
-            far_near.start()
-            side_near.start()
-            third_x.start()
-
-        @pl.when(jnp.logical_not(is_inner))
-        def _():
-            token_in(3).wait_recv()
-            second_x.start()
+            side_near(0).start()
+            side_near(1).start()
 
     def third_arrivals():
-        @pl.when(jnp.logical_not(is_inner))
-        def _():
-            token_in(5).wait_recv()
-            third_x.start()
-
-        token_in(4).wait_recv()
+        for p in range(2):
+            @pl.when(jnp.logical_not(is_inner))
+            def _():
+                token_in(5, p).wait_recv()
+                third_x(p).start()
+
+        token_in(4, 0).wait_recv()
+        token_in(4, 1).wait_recv()
 
     def stage_a(u):
         @pl.when(u >= 6)
         def _():
-            token_in(u).wait_recv()
+            token_in(u, 0).wait_recv()
+            token_in(u, 1).wait_recv()
 
         block = got[u]
         core_out[u] = jnp.dot(block, upv[1], preferred_element_type=F32).astype(BF16)
@@ -263,7 +285,10 @@
         @pl.when(u == 1)
         def _():
             z_out[1] = result.astype(BF16)
-            z_copy(1).start()
+
+            @pl.when(jnp.logical_not(is_inner))
+            def _():
+                z_copy(1).start()
 
         @pl.when(u == 2)
         def _():
@@ -285,6 +310,18 @@
         z_copy(d).start()
 
     def step(t, carry):
+        @pl.when((t >= 3) & (t < UNITS + 3))
+        def _():
+            stage_d(t - 3)
+
+        @pl.when((t >= 2) & (t < UNITS + 2))
+        def _():
+            stage_c(t - 2)
+
+        @pl.when((t >= 1) & (t < UNITS + 1))
+        def _():
+            stage_b(t - 1)
+
         @pl.when(t == 1)
         def _():
             first_arrivals()
@@ -297,22 +334,14 @@
         def _():
             third_arrivals()
 
+        @pl.when((t == 7) & is_inner)
+        def _():
+            z_copy(1).start()
+
         @pl.when(t < UNITS)
         def _():
             stage_a(t)
 
-        @pl.when((t >= 1) & (t < UNITS + 1))
-        def _():
-            stage_b(t - 1)
-
-        @pl.when((t >= 2) & (t < UNITS + 2))
-        def _():
-            stage_c(t - 2)
-
-        @pl.when((t >= 3) & (t < UNITS + 3))
-        def _():
-            stage_d(t - 3)
-
         @pl.when(t == 8)
         def _():
             stage_e(second)
@@ -321,37 +350,40 @@
 
     lax.fori_loop(0, UNITS + 3, step, 0)
 
-    stage_e(third)
-    over_copy().wait_recv()
-    x_out[0] = (over[0].astype(F32) + over[2].astype(F32)).astype(BF16)
-    x_copy(0).start()
-
-    x_copy(0).wait_recv()
-    total = acc[0] + x_in[0].astype(F32)
-    for d in range(1, NZ):
-        z_copy(d).wait_recv()
-        total = total + z_in[d].astype(F32)
-    out[...] = total.astype(BF16)
-
-    for copy in (own_x, own_near, side_near, second_x, third_x, over_copy()):
-        copy.wait_send()
+    for p in range(2):
+        for copy in (own_x, own_near, side_near, second_x, third_x):
+            copy(p).wait_send()
 
     @pl.when(is_inner)
     def _():
-        for copy in (own_across, near_across, far_near, across_near):
-            copy.wait_send()
-
-    for d in range(NZ):
-        if d:
-            z_copy(d).wait_send()
-        if d != 1:
-            x_copy(d).wait_send()
+        for p in range(2):
+            for copy in (own_across, near_across, far_near, across_near):
+                copy(p).wait_send()
+
     for u in range(UNITS):
         if u:
             weight(u).wait_send()
         core_copy(u).wait_send()
         y_copy(u).wait_send()
         hid_copy(u).wait_send()
+
+    stage_e(third)
+    over_copy().wait_recv()
+    x_out[0] = (over[0].astype(F32) + over[2].astype(F32)).astype(BF16)
+    x_copy(0).start()
+    over_copy().wait_send()
+    for d in range(1, NZ):
+        z_copy(d).wait_send()
+    x_copy(2).wait_send()
+    x_copy(3).wait_send()
+
+    total = acc[0]
+    for d in range(1, NZ):
+        z_copy(d).wait_recv()
+        total = total + z_in[d].astype(F32)
+    x_copy(0).wait_recv()
+    out[...] = (total + x_in[0].astype(F32)).astype(BF16)
+    x_copy(0).wait_send()
 
 
 def dense(tokens, route_ids, gate_scores, up_weight, down_weight):
@@ -383,7 +415,7 @@
             pltpu.VMEM((NZ, rows, features), BF16),
             pltpu.VMEM((NZ, rows, features), BF16),
             pltpu.VMEM((NZ, rows, features), BF16),
-        ] + [dma((9,))] + [dma((UNITS,))] * 9 + [dma((NZ,))] * 4 + [dma((5,))],
+        ] + [dma((9, 2)), dma((UNITS, 2))] + [dma((UNITS,))] * 8 + [dma((NZ,))] * 4 + [dma((5,))],
         compiler_params=pltpu.CompilerParams(
             collective_id=0, has_side_effects=True, vmem_limit_bytes=63 * 2**20
         ),

time: 65.3 us -> 70.1 us (1.074)
  Pallas kernels: 63.4 us -> 68.2 us
    pallas_call x1, Pallas kernels: 63.4 us -> 68.2 us  [dense(): pl.pallas_call(dense_kernel, out_shape=jax.ShapeDtypeStruct((rows, featur...]
where the time goes in v4:
time: 70.1 us; the launch traced here: 69.9 us
  Pallas kernels  68.2 us (97%)
  local copies, waits for them, and re-layouts  1.65 us (2%)
    pallas_call x1, Pallas kernels, dense(): pl.pallas_call(dense_kernel, out_shape=jax.ShapeDtypeStruct((rows, featur...  68.2 us
    unnamed x1, local copies, waits for them, and re-layouts  1.65 us

profile of v4, /device:TPU:0, one launch (start us, length us, event | category | flops | bytes accessed | tf_op | source)
XLA Modules:
  0.0 69.9 jit_solution(2308981596584335646)
XLA Ops:
  0.0 68.2 %shard_map.55 = bf16[128,896]{1,0:T(8,128)(2,1)} custom-call(bf16[128,896]{1,0:T(8,128)(2,1)} %tokens.1, s32[8,128]{1,0:T(8,128)} %bitcast.2, f32[8,128]{1,0:T(8,128)} %bitcast.3, bf16[1,896,1024]{2,1,0:T(8,128)(2,1)} %up.1, bf16[1,1024,896]{2,1,0:T(8,128)(2,1)} %down.1), custom_call_target="tpu_custom_call" | custom-call | flops 3758096384 | bytes 4128768 | tf_op jit(solution)/shard_map/pallas_call | solution.py:396
  68.2 1.6 %copy.7 = bf16[128,896]{1,0:T(8,128)(2,1)} copy(bf16[128,896]{1,0:T(8,128)(2,1)} %shard_map.55) | data formatting | bytes 458752

commit v5 on v3

--- a/solution.py
+++ b/solution.py
@@ -73,7 +73,7 @@
 
 def dense_kernel(
     tokens, route, gate, up, down, out,
-    got, upv, downv, wt, core_out, core_in, kept, y_out, y_in, hid, acc, over, x_out, x_in, z_out, z_in,
+    got, upv, downv, wt, core_out, core_in, kept, y_out, y_in, hid, hid_in, acc, res, over, x_out, x_in, z_out, z_in,
     tok_s, tok_r, w_s, w_r, core_s, core_r, y_s, y_r, hid_s, hid_r, x_s, x_r, z_s, z_r, load,
 ):
     expert = lax.axis_index("expert")
@@ -124,14 +124,15 @@
     def weight_in(u):
         return remote(wt.at[0], wt.at[u], w_s.at[u], w_r.at[u], x_peer)
 
-    def core_copy(u):
-        return remote(core_out.at[u], core_in.at[u], core_s.at[u], core_r.at[u], core_peer)
+    def core_copy(g):
+        pair = pl.ds(2 * g, 2)
+        return remote(core_out.at[pair], core_in.at[pair], core_s.at[g], core_r.at[g], core_peer)
 
     def y_copy(u):
         return remote(y_out.at[u], y_in.at[u], y_s.at[u], y_r.at[u], y_peer)
 
     def hid_copy(u):
-        return remote(hid.at[u, 0], hid.at[u, 1], hid_s.at[u], hid_r.at[u], core_peer)
+        return remote(hid.at[u], hid_in.at[u], hid_s.at[u], hid_r.at[u], core_peer)
 
     def x_copy(d):
         return remote(x_out.at[d], x_in.at[d], x_s.at[d], x_r.at[d], x_peer)
@@ -180,160 +181,158 @@
     for copy in loads:
         copy.wait()
 
-    def first_arrivals():
-        token_in(1).wait_recv()
-
-        @pl.when(is_inner)
-        def _():
-            near_across.start()
-            token_in(3).wait_recv()
-            across_near.start()
-            second_x.start()
-
-        token_in(2).wait_recv()
-
-        @pl.when(jnp.logical_not(is_inner))
-        def _():
-            side_near.start()
-
-    def second_arrivals():
-        @pl.when(is_inner)
-        def _():
-            token_in(5).wait_recv()
-            far_near.start()
-            side_near.start()
-            third_x.start()
-
-        @pl.when(jnp.logical_not(is_inner))
-        def _():
-            token_in(3).wait_recv()
-            second_x.start()
-
-    def third_arrivals():
-        @pl.when(jnp.logical_not(is_inner))
-        def _():
-            token_in(5).wait_recv()
-            third_x.start()
-
-        token_in(4).wait_recv()
-
-    def stage_a(u):
-        @pl.when(u >= 6)
-        def _():
-            token_in(u).wait_recv()
-
-        block = got[u]
-        core_out[u] = jnp.dot(block, upv[1], preferred_element_type=F32).astype(BF16)
-        core_copy(u).start()
-        kept[u] = jnp.dot(block, upv[0], preferred_element_type=F32)
-
-    def stage_b(u):
-        core_copy(u).wait_recv()
-        total = kept[u] + core_in[u].astype(F32)
-        kept[u] = total
-        y_out[u] = total.astype(BF16)
-        y_copy(u).start()
-
-    def stage_c(u):
-        y_copy(u).wait_recv()
-        before = kept[u] + y_in[u].astype(F32)
-        hid[u, 0] = (before / (1.0 + jnp.exp(-before))).astype(BF16)
-        hid_copy(u).start()
-
-    def stage_d(u):
-        other = (u == 2) | (u == 4) | (u >= 6)
-        d = jnp.where((u == 1) | (u == 6), 1, jnp.where((u == 3) | (u == 4), second, third))
-        d = jnp.where((u == 0) | (u == 2), 0, d)
-        k = 2 * d + other.astype(jnp.int32)
+    def arrivals(g):
+        @pl.when(g == 0)
+        def _():
+            token_in(1).wait_recv()
+
+            @pl.when(is_inner)
+            def _():
+                near_across.start()
+                token_in(3).wait_recv()
+                across_near.start()
+                second_x.start()
+
+        @pl.when(g == 1)
+        def _():
+            token_in(2).wait_recv()
+
+            @pl.when(is_inner)
+            def _():
+                token_in(5).wait_recv()
+                far_near.start()
+                side_near.start()
+                third_x.start()
+
+            @pl.when(jnp.logical_not(is_inner))
+            def _():
+                side_near.start()
+                token_in(3).wait_recv()
+                second_x.start()
+
+        @pl.when(g == 2)
+        def _():
+            @pl.when(jnp.logical_not(is_inner))
+            def _():
+                token_in(5).wait_recv()
+                third_x.start()
+
+            token_in(4).wait_recv()
+
+        @pl.when(g == 3)
+        def _():
+            token_in(6).wait_recv()
+            token_in(7).wait_recv()
+
+    def stage_a(g):
+        pair = pl.ds(2 * g, 2)
+        block = got[pair].reshape(2 * rows, got.shape[2])
+        theirs_sum = jnp.dot(block, upv[1], preferred_element_type=F32)
+        core_out[pair] = theirs_sum.astype(BF16).reshape(2, rows, half)
+        core_copy(g).start()
+        kept[pair] = jnp.dot(block, upv[0], preferred_element_type=F32).reshape(2, rows, half)
+
+    def stage_b(g):
+        core_copy(g).wait_recv()
+        for u in (2 * g, 2 * g + 1):
+            total = kept[u] + core_in[u].astype(F32)
+            kept[u] = total
+            y_out[u] = total.astype(BF16)
+            y_copy(u).start()
+
+    def stage_c(g):
+        for u in (2 * g, 2 * g + 1):
+            y_copy(u).wait_recv()
+            before = kept[u] + y_in[u].astype(F32)
+            hid[u] = (before / (1.0 + jnp.exp(-before))).astype(BF16)
+            hid_copy(u).start()
+
+    places = [0, 2, 1, 2 * second, 2 * second + 1, 2 * third, 3, 2 * third + 1]
+
+    def scale_of(u):
+        k = places[7]
+        for position in range(UNITS - 1):
+            k = jnp.where(u == position, places[position], k)
 
         @pl.when(u >= 1)
         def _():
             weight_in(k).wait_recv()
 
-        scale = jnp.broadcast_to(wt[k, pl.ds(expert, 1), :], (128, rows)).T
-        hid_copy(u).wait_recv()
-        result = jnp.dot(hid[u, 0], downv[0], preferred_element_type=F32)
-        result = result + jnp.dot(hid[u, 1], downv[1], preferred_element_type=F32)
-        result = result * jnp.concatenate([scale] * (result.shape[1] // 128), axis=1)
-
-        @pl.when((u == 0) | (u == 3) | (u == 5))
-        def _():
-            acc[d] = result
-
-        @pl.when(u == 1)
-        def _():
-            z_out[1] = result.astype(BF16)
-            z_copy(1).start()
-
-        @pl.when(u == 2)
-        def _():
-            over[0] = result.astype(BF16)
-
-        @pl.when(u == 6)
-        def _():
-            over[1] = result.astype(BF16)
+        return jnp.broadcast_to(wt[k, pl.ds(expert, 1), :], (128, rows)).T
+
+    def stage_d(g):
+        pair = pl.ds(2 * g, 2)
+        scale = jnp.concatenate([scale_of(2 * g), scale_of(2 * g + 1)], axis=0)
+        hid_copy(2 * g).wait_recv()
+        hid_copy(2 * g + 1).wait_recv()
+        columns = res.shape[2]
+        result = jnp.dot(hid[pair].reshape(2 * rows, half), downv[0], preferred_element_type=F32)
+        result = result + jnp.dot(hid_in[pair].reshape(2 * rows, half), downv[1], preferred_element_type=F32)
+        result = result * jnp.concatenate([scale] * (columns // 128), axis=1)
+        res[...] = result.reshape(2, rows, columns)
+
+        @pl.when(g == 0)
+        def _():
+            z_out[1] = res[1].astype(BF16)
+
+            @pl.when(jnp.logical_not(is_inner))
+            def _():
+                z_copy(1).start()
+
+            acc[0] = res[0]
+
+        @pl.when(g == 1)
+        def _():
+            over[0] = res[0].astype(BF16)
+            acc[second] = res[1]
+
+        @pl.when(g == 2)
+        def _():
+            x_out[second] = res[0].astype(BF16)
+            x_copy(second).start()
+            acc[third] = res[1]
+
+        @pl.when(g == 3)
+        def _():
+            x_out[third] = res[1].astype(BF16)
+            x_copy(third).start()
+            over[1] = res[0].astype(BF16)
             over_copy().start()
-
-        @pl.when((u == 4) | (u == 7))
-        def _():
-            x_out[d] = result.astype(BF16)
-            x_copy(d).start()
 
     def stage_e(d):
         x_copy(d).wait_recv()
         z_out[d] = (acc[d] + x_in[d].astype(F32)).astype(BF16)
         z_copy(d).start()
 
+    pairs = UNITS // 2
+
     def step(t, carry):
-        @pl.when(t == 1)
-        def _():
-            first_arrivals()
-
-        @pl.when(t == 3)
-        def _():
-            second_arrivals()
-
-        @pl.when(t == 4)
-        def _():
-            third_arrivals()
-
-        @pl.when(t < UNITS)
-        def _():
+        @pl.when(t < pairs)
+        def _():
+            arrivals(t)
             stage_a(t)
-
-        @pl.when((t >= 1) & (t < UNITS + 1))
-        def _():
-            stage_b(t - 1)
-
-        @pl.when((t >= 2) & (t < UNITS + 2))
-        def _():
-            stage_c(t - 2)
-
-        @pl.when((t >= 3) & (t < UNITS + 3))
-        def _():
-            stage_d(t - 3)
-
-        @pl.when(t == 8)
-        def _():
-            stage_e(second)
+            stage_b(t)
+
+        @pl.when((t == 3) & is_inner)
+        def _():
+            z_copy(1).start()
+
+        @pl.when(t >= 1)
+        def _():
+            stage_c(t - 1)
+            stage_d(t - 1)
 
         return carry
 
-    lax.fori_loop(0, UNITS + 3, step, 0)
-
+    lax.fori_loop(0, pairs + 1, step, 0)
+
+    stage_e(second)
     stage_e(third)
     over_copy().wait_recv()
     x_out[0] = (over[0].astype(F32) + over[2].astype(F32)).astype(BF16)
     x_copy(0).start()
 
-    x_copy(0).wait_recv()
-    total = acc[0] + x_in[0].astype(F32)
-    for d in range(1, NZ):
-        z_copy(d).wait_recv()
-        total = total + z_in[d].astype(F32)
-    out[...] = total.astype(BF16)
-
-    for copy in (own_x, own_near, side_near, second_x, third_x, over_copy()):
+    for copy in (own_x, own_near, side_near, second_x, third_x):
         copy.wait_send()
 
     @pl.when(is_inner)
@@ -341,17 +340,26 @@
         for copy in (own_across, near_across, far_near, across_near):
             copy.wait_send()
 
-    for d in range(NZ):
-        if d:
-            z_copy(d).wait_send()
-        if d != 1:
-            x_copy(d).wait_send()
     for u in range(UNITS):
         if u:
             weight(u).wait_send()
-        core_copy(u).wait_send()
         y_copy(u).wait_send()
         hid_copy(u).wait_send()
+    for g in range(pairs):
+        core_copy(g).wait_send()
+    over_copy().wait_send()
+    for d in range(1, NZ):
+        z_copy(d).wait_send()
+    x_copy(2).wait_send()
+    x_copy(3).wait_send()
+
+    total = acc[0]
+    for d in range(1, NZ):
+        z_copy(d).wait_recv()
+        total = total + z_in[d].astype(F32)
+    x_copy(0).wait_recv()
+    out[...] = (total + x_in[0].astype(F32)).astype(BF16)
+    x_copy(0).wait_send()
 
 
 def dense(tokens, route_ids, gate_scores, up_weight, down_weight):
@@ -376,8 +384,10 @@
             pltpu.VMEM((UNITS, rows, half), F32),
             pltpu.VMEM((UNITS, rows, half), BF16),
             pltpu.VMEM((UNITS, rows, half), BF16),
-            pltpu.VMEM((UNITS, 2, rows, half), BF16),
+            pltpu.VMEM((UNITS, rows, half), BF16),
+            pltpu.VMEM((UNITS, rows, half), BF16),
             pltpu.VMEM((NZ, rows, features), F32),
+            pltpu.VMEM((2, rows, features), F32),
             pltpu.VMEM((3, rows, features), BF16),
             pltpu.VMEM((NZ, rows, features), BF16),
             pltpu.VMEM((NZ, rows, features), BF16),

time: 65.3 us -> 68.9 us (1.055)
  Pallas kernels: 63.4 us -> 67.1 us
    pallas_call x1, Pallas kernels: 63.4 us -> 67.1 us  [dense(): pl.pallas_call(dense_kernel, out_shape=jax.ShapeDtypeStruct((rows, featur...]
where the time goes in v5:
time: 68.9 us; the launch traced here: 68.7 us
  Pallas kernels  67.1 us (97%)
  local copies, waits for them, and re-layouts  1.65 us (2%)
    pallas_call x1, Pallas kernels, dense(): pl.pallas_call(dense_kernel, out_shape=jax.ShapeDtypeStruct((rows, featur...  67.1 us
    unnamed x1, local copies, waits for them, and re-layouts  1.65 us

profile of v5, /device:TPU:0, one launch (start us, length us, event | category | flops | bytes accessed | tf_op | source)
XLA Modules:
  0.0 68.7 jit_solution(6773818998719070350)
XLA Ops:
  0.0 67.1 %shard_map.55 = bf16[128,896]{1,0:T(8,128)(2,1)} custom-call(bf16[128,896]{1,0:T(8,128)(2,1)} %tokens.1, s32[8,128]{1,0:T(8,128)} %bitcast.2, f32[8,128]{1,0:T(8,128)} %bitcast.3, bf16[1,896,1024]{2,1,0:T(8,128)(2,1)} %up.1, bf16[1,1024,896]{2,1,0:T(8,128)(2,1)} %down.1), custom_call_target="tpu_custom_call" | custom-call | flops 3758096384 | bytes 4128768 | tf_op jit(solution)/shard_map/pallas_call | solution.py:372
  67.1 1.6 %copy.7 = bf16[128,896]{1,0:T(8,128)(2,1)} copy(bf16[128,896]{1,0:T(8,128)(2,1)} %shard_map.55) | data formatting | bytes 458752

commit v6 on v3

--- a/solution.py
+++ b/solution.py
@@ -73,7 +73,7 @@
 
 def dense_kernel(
     tokens, route, gate, up, down, out,
-    got, upv, downv, wt, core_out, core_in, kept, y_out, y_in, hid, acc, over, x_out, x_in, z_out, z_in,
+    got, upv, downv, wt, core_out, core_in, kept, y_out, y_in, hid, acc, x_out, x_in, z_out, z_in,
     tok_s, tok_r, w_s, w_r, core_s, core_r, y_s, y_r, hid_s, hid_r, x_s, x_r, z_s, z_r, load,
 ):
     expert = lax.axis_index("expert")
@@ -135,9 +135,6 @@
 
     def x_copy(d):
         return remote(x_out.at[d], x_in.at[d], x_s.at[d], x_r.at[d], x_peer)
-
-    def over_copy():
-        return remote(over.at[1], over.at[2], z_s.at[0], z_r.at[0], near)
 
     def z_copy(d):
         return remote(z_out.at[d], z_in.at[d], z_s.at[d], z_r.at[d], at(d, False))
@@ -256,25 +253,11 @@
         result = result + jnp.dot(hid[u, 1], downv[1], preferred_element_type=F32)
         result = result * jnp.concatenate([scale] * (result.shape[1] // 128), axis=1)
 
-        @pl.when((u == 0) | (u == 3) | (u == 5))
+        @pl.when(jnp.logical_not(other))
         def _():
             acc[d] = result
 
-        @pl.when(u == 1)
-        def _():
-            z_out[1] = result.astype(BF16)
-            z_copy(1).start()
-
-        @pl.when(u == 2)
-        def _():
-            over[0] = result.astype(BF16)
-
-        @pl.when(u == 6)
-        def _():
-            over[1] = result.astype(BF16)
-            over_copy().start()
-
-        @pl.when((u == 4) | (u == 7))
+        @pl.when(other)
         def _():
             x_out[d] = result.astype(BF16)
             x_copy(d).start()
@@ -285,10 +268,6 @@
         z_copy(d).start()
 
     def step(t, carry):
-        @pl.when(t == 1)
-        def _():
-            first_arrivals()
-
         @pl.when(t == 3)
         def _():
             second_arrivals()
@@ -301,7 +280,7 @@
         def _():
             stage_a(t)
 
-        @pl.when((t >= 1) & (t < UNITS + 1))
+        @pl.when((t >= 2) & (t < UNITS + 1))
         def _():
             stage_b(t - 1)
 
@@ -319,21 +298,15 @@
 
         return carry
 
-    lax.fori_loop(0, UNITS + 3, step, 0)
-
+    stage_a(0)
+    stage_b(0)
+    first_arrivals()
+    lax.fori_loop(1, UNITS + 3, step, 0)
+
+    stage_e(1)
     stage_e(third)
-    over_copy().wait_recv()
-    x_out[0] = (over[0].astype(F32) + over[2].astype(F32)).astype(BF16)
-    x_copy(0).start()
-
-    x_copy(0).wait_recv()
-    total = acc[0] + x_in[0].astype(F32)
-    for d in range(1, NZ):
-        z_copy(d).wait_recv()
-        total = total + z_in[d].astype(F32)
-    out[...] = total.astype(BF16)
-
-    for copy in (own_x, own_near, side_near, second_x, third_x, over_copy()):
+
+    for copy in (own_x, own_near, side_near, second_x, third_x):
         copy.wait_send()
 
     @pl.when(is_inner)
@@ -341,17 +314,23 @@
         for copy in (own_across, near_across, far_near, across_near):
             copy.wait_send()
 
-    for d in range(NZ):
-        if d:
-            z_copy(d).wait_send()
-        if d != 1:
-            x_copy(d).wait_send()
     for u in range(UNITS):
         if u:
             weight(u).wait_send()
         core_copy(u).wait_send()
         y_copy(u).wait_send()
         hid_copy(u).wait_send()
+    for d in range(NZ):
+        x_copy(d).wait_send()
+
+    x_copy(0).wait_recv()
+    total = acc[0] + x_in[0].astype(F32)
+    for d in (1, 2, 3):
+        z_copy(d).wait_send()
+    for d in (1, 2, 3):
+        z_copy(d).wait_recv()
+        total = total + z_in[d].astype(F32)
+    out[...] = total.astype(BF16)
 
 
 def dense(tokens, route_ids, gate_scores, up_weight, down_weight):
@@ -378,7 +357,6 @@
             pltpu.VMEM((UNITS, rows, half), BF16),
             pltpu.VMEM((UNITS, 2, rows, half), BF16),
             pltpu.VMEM((NZ, rows, features), F32),
-            pltpu.VMEM((3, rows, features), BF16),
             pltpu.VMEM((NZ, rows, features), BF16),
             pltpu.VMEM((NZ, rows, features), BF16),
             pltpu.VMEM((NZ, rows, features), BF16),

time: 65.3 us -> 66.4 us (1.017)
  Pallas kernels: 63.4 us -> 64.5 us
    pallas_call x1, Pallas kernels: 63.4 us -> 64.5 us  [dense(): pl.pallas_call(dense_kernel, out_shape=jax.ShapeDtypeStruct((rows, featur...]
where the time goes in v6:
time: 66.4 us; the launch traced here: 66.1 us
  Pallas kernels  64.5 us (97%)
  local copies, waits for them, and re-layouts  1.65 us (2%)
    pallas_call x1, Pallas kernels, dense(): pl.pallas_call(dense_kernel, out_shape=jax.ShapeDtypeStruct((rows, featur...  64.5 us
    unnamed x1, local copies, waits for them, and re-layouts  1.65 us

profile of v6, /device:TPU:0, one launch (start us, length us, event | category | flops | bytes accessed | tf_op | source)
XLA Modules:
  0.0 66.1 jit_solution(11641763495588989422)
XLA Ops:
  0.0 64.5 %shard_map.55 = bf16[128,896]{1,0:T(8,128)(2,1)} custom-call(bf16[128,896]{1,0:T(8,128)(2,1)} %tokens.1, s32[8,128]{1,0:T(8,128)} %bitcast.2, f32[8,128]{1,0:T(8,128)} %bitcast.3, bf16[1,896,1024]{2,1,0:T(8,128)(2,1)} %up.1, bf16[1,1024,896]{2,1,0:T(8,128)(2,1)} %down.1), custom_call_target="tpu_custom_call" | custom-call | flops 3758096384 | bytes 4128768 | tf_op jit(solution)/shard_map/pallas_call | solution.py:343
  64.5 1.6 %copy.7 = bf16[128,896]{1,0:T(8,128)(2,1)} copy(bf16[128,896]{1,0:T(8,128)(2,1)} %shard_map.55) | data formatting | bytes 458752

commit v7 on v4

--- a/solution.py
+++ b/solution.py
@@ -101,17 +101,14 @@
     is_inner = inner == 1
     near, across = at(1, False), at(3, False)
 
-    part_rows = rows // 2
-
     def token(k, src, slot, device):
         def piece(p):
-            lines = pl.ds(p * part_rows, part_rows)
-            return remote(src.at[lines], got.at[slot, lines], tok_s.at[k, p], tok_r.at[slot, p], device)
+            return remote(
+                src.at[lines(p)], got.at[slot, lines(p)], tok_s.at[k, p], tok_r.at[slot, p], device)
         return piece
 
     def token_in(u, p):
-        lines = pl.ds(p * part_rows, part_rows)
-        return remote(tokens.at[lines], got.at[u, lines], tok_s.at[0, p], tok_r.at[u, p], x_peer)
+        return remote(tokens.at[lines(p)], got.at[u, lines(p)], tok_s.at[0, p], tok_r.at[u, p], x_peer)
 
     second, third = 2 + inner, 3 - inner
     own_x = token(0, tokens, 2, x_peer)
@@ -139,14 +136,19 @@
     def hid_copy(u):
         return remote(hid.at[u, 0], hid.at[u, 1], hid_s.at[u], hid_r.at[u], core_peer)
 
-    def x_copy(d):
-        return remote(x_out.at[d], x_in.at[d], x_s.at[d], x_r.at[d], x_peer)
-
-    def over_copy():
-        return remote(over.at[1], over.at[2], z_s.at[0], z_r.at[0], near)
-
-    def z_copy(d):
-        return remote(z_out.at[d], z_in.at[d], z_s.at[d], z_r.at[d], at(d, False))
+    part_rows = rows // 2
+
+    def lines(p):
+        return pl.ds(p * part_rows, part_rows)
+
+    def x_copy(d, p):
+        return remote(x_out.at[d, lines(p)], x_in.at[d, lines(p)], x_s.at[d, p], x_r.at[d, p], x_peer)
+
+    def over_copy(p):
+        return remote(over.at[1, lines(p)], over.at[2, lines(p)], z_s.at[0, p], z_r.at[0, p], near)
+
+    def z_copy(d, p):
+        return remote(z_out.at[d, lines(p)], z_in.at[d, lines(p)], z_s.at[d, p], z_r.at[d, p], at(d, False))
 
     own = pl.ds(pl.multiple_of(core * half, half), half)
     theirs = pl.ds(pl.multiple_of((1 - core) * half, half), half)
@@ -285,10 +287,8 @@
         @pl.when(u == 1)
         def _():
             z_out[1] = result.astype(BF16)
-
-            @pl.when(jnp.logical_not(is_inner))
-            def _():
-                z_copy(1).start()
+            z_copy(1, 0).start()
+            z_copy(1, 1).start()
 
         @pl.when(u == 2)
         def _():
@@ -297,58 +297,56 @@
         @pl.when(u == 6)
         def _():
             over[1] = result.astype(BF16)
-            over_copy().start()
+            over_copy(0).start()
+            over_copy(1).start()
 
         @pl.when((u == 4) | (u == 7))
         def _():
             x_out[d] = result.astype(BF16)
-            x_copy(d).start()
-
-    def stage_e(d):
-        x_copy(d).wait_recv()
-        z_out[d] = (acc[d] + x_in[d].astype(F32)).astype(BF16)
-        z_copy(d).start()
+            x_copy(d, 0).start()
+            x_copy(d, 1).start()
+
+    def stage_e(d, p):
+        x_copy(d, p).wait_recv()
+        z_out[d, lines(p)] = (acc[d, lines(p)] + x_in[d, lines(p)].astype(F32)).astype(BF16)
+        z_copy(d, p).start()
 
     def step(t, carry):
+        @pl.when(t == 3)
+        def _():
+            second_arrivals()
+
+        @pl.when(t == 4)
+        def _():
+            third_arrivals()
+
+        @pl.when(t < UNITS)
+        def _():
+            stage_a(t)
+
+        @pl.when((t >= 2) & (t < UNITS + 1))
+        def _():
+            stage_b(t - 1)
+
+        @pl.when((t >= 2) & (t < UNITS + 2))
+        def _():
+            stage_c(t - 2)
+
         @pl.when((t >= 3) & (t < UNITS + 3))
         def _():
             stage_d(t - 3)
 
-        @pl.when((t >= 2) & (t < UNITS + 2))
-        def _():
-            stage_c(t - 2)
-
-        @pl.when((t >= 1) & (t < UNITS + 1))
-        def _():
-            stage_b(t - 1)
-
-        @pl.when(t == 1)
-        def _():
-            first_arrivals()
-
-        @pl.when(t == 3)
-        def _():
-            second_arrivals()
-
-        @pl.when(t == 4)
-        def _():
-            third_arrivals()
-
-        @pl.when((t == 7) & is_inner)
-        def _():
-            z_copy(1).start()
-
-        @pl.when(t < UNITS)
-        def _():
-            stage_a(t)
-
         @pl.when(t == 8)
         def _():
-            stage_e(second)
+            stage_e(second, 0)
+            stage_e(second, 1)
 
         return carry
 
-    lax.fori_loop(0, UNITS + 3, step, 0)
+    stage_a(0)
+    stage_b(0)
+    first_arrivals()
+    lax.fori_loop(1, UNITS + 3, step, 0)
 
     for p in range(2):
         for copy in (own_x, own_near, side_near, second_x, third_x):
@@ -367,23 +365,28 @@
         y_copy(u).wait_send()
         hid_copy(u).wait_send()
 
-    stage_e(third)
-    over_copy().wait_recv()
-    x_out[0] = (over[0].astype(F32) + over[2].astype(F32)).astype(BF16)
-    x_copy(0).start()
-    over_copy().wait_send()
-    for d in range(1, NZ):
-        z_copy(d).wait_send()
-    x_copy(2).wait_send()
-    x_copy(3).wait_send()
-
-    total = acc[0]
-    for d in range(1, NZ):
-        z_copy(d).wait_recv()
-        total = total + z_in[d].astype(F32)
-    x_copy(0).wait_recv()
-    out[...] = (total + x_in[0].astype(F32)).astype(BF16)
-    x_copy(0).wait_send()
+    for p in range(2):
+        stage_e(third, p)
+        over_copy(p).wait_recv()
+        x_out[0, lines(p)] = (over[0, lines(p)].astype(F32) + over[2, lines(p)].astype(F32)).astype(BF16)
+        x_copy(0, p).start()
+
+    for p in range(2):
+        over_copy(p).wait_send()
+        x_copy(2, p).wait_send()
+        x_copy(3, p).wait_send()
+        for d in range(1, NZ):
+            z_copy(d, p).wait_send()
+
+    for p in range(2):
+        total = acc[0, lines(p)]
+        for d in range(1, NZ):
+            z_copy(d, p).wait_recv()
+            total = total + z_in[d, lines(p)].astype(F32)
+        x_copy(0, p).wait_recv()
+        out[lines(p)] = (total + x_in[0, lines(p)].astype(F32)).astype(BF16)
+    for p in range(2):
+        x_copy(0, p).wait_send()
 
 
 def dense(tokens, route_ids, gate_scores, up_weight, down_weight):
@@ -415,7 +418,7 @@
             pltpu.VMEM((NZ, rows, features), BF16),
             pltpu.VMEM((NZ, rows, features), BF16),
             pltpu.VMEM((NZ, rows, features), BF16),
-        ] + [dma((9, 2)), dma((UNITS, 2))] + [dma((UNITS,))] * 8 + [dma((NZ,))] * 4 + [dma((5,))],
+        ] + [dma((9, 2)), dma((UNITS, 2))] + [dma((UNITS,))] * 8 + [dma((NZ, 2))] * 4 + [dma((5,))],
         compiler_params=pltpu.CompilerParams(
             collective_id=0, has_side_effects=True, vmem_limit_bytes=63 * 2**20
         ),

time: 70.1 us -> 62.3 us (0.89)
  Pallas kernels: 68.2 us -> 60.4 us
    pallas_call x1, Pallas kernels: 68.2 us -> 60.4 us  [dense(): pl.pallas_call(dense_kernel, out_shape=jax.ShapeDtypeStruct((rows, featur...]
where the time goes in v7:
time: 62.3 us; the launch traced here: 62.1 us
  Pallas kernels  60.4 us (97%)
  local copies, waits for them, and re-layouts  1.65 us (3%)
    pallas_call x1, Pallas kernels, dense(): pl.pallas_call(dense_kernel, out_shape=jax.ShapeDtypeStruct((rows, featur...  60.4 us
    unnamed x1, local copies, waits for them, and re-layouts  1.65 us

profile of v7, /device:TPU:0, one launch (start us, length us, event | category | flops | bytes accessed | tf_op | source)
XLA Modules:
  0.0 62.1 jit_solution(15845960855967030568)
XLA Ops:
  0.0 60.4 %shard_map.55 = bf16[128,896]{1,0:T(8,128)(2,1)} custom-call(bf16[128,896]{1,0:T(8,128)(2,1)} %tokens.1, s32[8,128]{1,0:T(8,128)} %bitcast.2, f32[8,128]{1,0:T(8,128)} %bitcast.3, bf16[1,896,1024]{2,1,0:T(8,128)(2,1)} %up.1, bf16[1,1024,896]{2,1,0:T(8,128)(2,1)} %down.1), custom_call_target="tpu_custom_call" | custom-call | flops 3758096384 | bytes 4128768 | tf_op jit(solution)/shard_map/pallas_call | solution.py:399
  60.4 1.6 %copy.7 = bf16[128,896]{1,0:T(8,128)(2,1)} copy(bf16[128,896]{1,0:T(8,128)(2,1)} %shard_map.55) | data formatting | bytes 458752

commit v8 on v7

--- a/solution.py
+++ b/solution.py
@@ -120,6 +120,7 @@
     far_near = token(6, got.at[5], 5, near)
     second_x = token(7, got.at[3], 4, x_peer)
     third_x = token(8, got.at[5], 7, x_peer)
+    near_x = token(9, got.at[1], 6, x_peer)
 
     def weight(k):
         return remote(wt.at[0], wt.at[k], w_s.at[k], w_r.at[k], at(k // 2, k % 2 == 1))
@@ -206,11 +207,14 @@
                 across_near(p).start()
                 second_x(p).start()
 
+            if p == 1:
+                near_x(1).start()
             token_in(2, p).wait_recv()
 
-            @pl.when(jnp.logical_not(is_inner))
-            def _():
-                side_near(p).start()
+            if p == 0:
+                @pl.when(jnp.logical_not(is_inner))
+                def _():
+                    side_near(0).start()
 
     def second_arrivals():
         for p in range(2):
@@ -228,7 +232,6 @@
         @pl.when(is_inner)
         def _():
             side_near(0).start()
-            side_near(1).start()
 
     def third_arrivals():
         for p in range(2):
@@ -287,8 +290,11 @@
         @pl.when(u == 1)
         def _():
             z_out[1] = result.astype(BF16)
-            z_copy(1, 0).start()
-            z_copy(1, 1).start()
+
+            @pl.when(jnp.logical_not(is_inner))
+            def _():
+                z_copy(1, 0).start()
+                z_copy(1, 1).start()
 
         @pl.when(u == 2)
         def _():
@@ -336,6 +342,11 @@
         def _():
             stage_d(t - 3)
 
+        @pl.when((t == 7) & is_inner)
+        def _():
+            z_copy(1, 0).start()
+            z_copy(1, 1).start()
+
         @pl.when(t == 8)
         def _():
             stage_e(second, 0)
@@ -349,8 +360,10 @@
     lax.fori_loop(1, UNITS + 3, step, 0)
 
     for p in range(2):
-        for copy in (own_x, own_near, side_near, second_x, third_x):
+        for copy in (own_x, own_near, second_x, third_x):
             copy(p).wait_send()
+    side_near(0).wait_send()
+    near_x(1).wait_send()
 
     @pl.when(is_inner)
     def _():
@@ -418,7 +431,7 @@
             pltpu.VMEM((NZ, rows, features), BF16),
             pltpu.VMEM((NZ, rows, features), BF16),
             pltpu.VMEM((NZ, rows, features), BF16),
-        ] + [dma((9, 2)), dma((UNITS, 2))] + [dma((UNITS,))] * 8 + [dma((NZ, 2))] * 4 + [dma((5,))],
+        ] + [dma((10, 2)), dma((UNITS, 2))] + [dma((UNITS,))] * 8 + [dma((NZ, 2))] * 4 + [dma((5,))],
         compiler_params=pltpu.CompilerParams(
             collective_id=0, has_side_effects=True, vmem_limit_bytes=63 * 2**20
         ),

time: 62.3 us -> 62.2 us (level)
  no operation moved by 1% of the time
where the time goes in v8:
time: 62.2 us; the launch traced here: 62 us
  Pallas kernels  60.3 us (97%)
  local copies, waits for them, and re-layouts  1.65 us (3%)
    pallas_call x1, Pallas kernels, dense(): pl.pallas_call(dense_kernel, out_shape=jax.ShapeDtypeStruct((rows, featur...  60.3 us
    unnamed x1, local copies, waits for them, and re-layouts  1.65 us

profile of v8, /device:TPU:0, one launch (start us, length us, event | category | flops | bytes accessed | tf_op | source)
XLA Modules:
  0.0 62.0 jit_solution(12721661936333809429)
XLA Ops:
  0.0 60.3 %shard_map.55 = bf16[128,896]{1,0:T(8,128)(2,1)} custom-call(bf16[128,896]{1,0:T(8,128)(2,1)} %tokens.1, s32[8,128]{1,0:T(8,128)} %bitcast.2, f32[8,128]{1,0:T(8,128)} %bitcast.3, bf16[1,896,1024]{2,1,0:T(8,128)(2,1)} %up.1, bf16[1,1024,896]{2,1,0:T(8,128)(2,1)} %down.1), custom_call_target="tpu_custom_call" | custom-call | flops 3758096384 | bytes 4128768 | tf_op jit(solution)/shard_map/pallas_call | solution.py:412
  60.4 1.6 %copy.7 = bf16[128,896]{1,0:T(8,128)(2,1)} copy(bf16[128,896]{1,0:T(8,128)(2,1)} %shard_map.55) | data formatting | bytes 458752

commit v9 on v8

--- a/solution.py
+++ b/solution.py
@@ -334,13 +334,13 @@
         def _():
             stage_b(t - 1)
 
+        @pl.when((t >= 3) & (t < UNITS + 3))
+        def _():
+            stage_d(t - 3)
+
         @pl.when((t >= 2) & (t < UNITS + 2))
         def _():
             stage_c(t - 2)
-
-        @pl.when((t >= 3) & (t < UNITS + 3))
-        def _():
-            stage_d(t - 3)
 
         @pl.when((t == 7) & is_inner)
         def _():

time: 62.2 us -> 62 us (level)
  no operation moved by 1% of the time
where the time goes in v9:
time: 62 us; the launch traced here: 61.8 us
  Pallas kernels  60.1 us (97%)
  local copies, waits for them, and re-layouts  1.65 us (3%)
    pallas_call x1, Pallas kernels, dense(): pl.pallas_call(dense_kernel, out_shape=jax.ShapeDtypeStruct((rows, featur...  60.1 us
    unnamed x1, local copies, waits for them, and re-layouts  1.65 us

profile of v9, /device:TPU:0, one launch (start us, length us, event | category | flops | bytes accessed | tf_op | source)
XLA Modules:
  0.0 61.8 jit_solution(8060546353170368845)
XLA Ops:
  0.0 60.1 %shard_map.55 = bf16[128,896]{1,0:T(8,128)(2,1)} custom-call(bf16[128,896]{1,0:T(8,128)(2,1)} %tokens.1, s32[8,128]{1,0:T(8,128)} %bitcast.2, f32[8,128]{1,0:T(8,128)} %bitcast.3, bf16[1,896,1024]{2,1,0:T(8,128)(2,1)} %up.1, bf16[1,1024,896]{2,1,0:T(8,128)(2,1)} %down.1), custom_call_target="tpu_custom_call" | custom-call | flops 3758096384 | bytes 4128768 | tf_op jit(solution)/shard_map/pallas_call | solution.py:412
  60.1 1.6 %copy.7 = bf16[128,896]{1,0:T(8,128)(2,1)} copy(bf16[128,896]{1,0:T(8,128)(2,1)} %shard_map.55) | data formatting | bytes 458752

commit v10 on v8

--- a/solution.py
+++ b/solution.py
@@ -135,7 +135,7 @@
         return remote(y_out.at[u], y_in.at[u], y_s.at[u], y_r.at[u], y_peer)
 
     def hid_copy(u):
-        return remote(hid.at[u, 0], hid.at[u, 1], hid_s.at[u], hid_r.at[u], core_peer)
+        return remote(hid.at[u, :, :half], hid.at[u, :, half:], hid_s.at[u], hid_r.at[u], core_peer)
 
     part_rows = rows // 2
 
@@ -157,8 +157,8 @@
         pltpu.make_async_copy(tokens, got.at[0], load.at[0]),
         pltpu.make_async_copy(up.at[0, :, theirs], upv.at[1], load.at[1]),
         pltpu.make_async_copy(up.at[0, :, own], upv.at[0], load.at[2]),
-        pltpu.make_async_copy(down.at[0, own, :], downv.at[0], load.at[3]),
-        pltpu.make_async_copy(down.at[0, theirs, :], downv.at[1], load.at[4]),
+        pltpu.make_async_copy(down.at[0, own, :], downv.at[:half], load.at[3]),
+        pltpu.make_async_copy(down.at[0, theirs, :], downv.at[half:], load.at[4]),
     ]
     for copy in loads:
         copy.start()
@@ -264,7 +264,7 @@
     def stage_c(u):
         y_copy(u).wait_recv()
         before = kept[u] + y_in[u].astype(F32)
-        hid[u, 0] = (before / (1.0 + jnp.exp(-before))).astype(BF16)
+        hid[u, :, :half] = (before / (1.0 + jnp.exp(-before))).astype(BF16)
         hid_copy(u).start()
 
     def stage_d(u):
@@ -279,8 +279,7 @@
 
         scale = jnp.broadcast_to(wt[k, pl.ds(expert, 1), :], (128, rows)).T
         hid_copy(u).wait_recv()
-        result = jnp.dot(hid[u, 0], downv[0], preferred_element_type=F32)
-        result = result + jnp.dot(hid[u, 1], downv[1], preferred_element_type=F32)
+        result = jnp.dot(hid[u], downv[...], preferred_element_type=F32)
         result = result * jnp.concatenate([scale] * (result.shape[1] // 128), axis=1)
 
         @pl.when((u == 0) | (u == 3) | (u == 5))
@@ -417,14 +416,14 @@
         scratch_shapes=[
             pltpu.VMEM((UNITS, rows, features), BF16),
             pltpu.VMEM((2, features, half), BF16),
-            pltpu.VMEM((2, half, features), BF16),
+            pltpu.VMEM((hidden, features), BF16),
             pltpu.VMEM((UNITS, UNITS, rows), F32),
             pltpu.VMEM((UNITS, rows, half), BF16),
             pltpu.VMEM((UNITS, rows, half), BF16),
             pltpu.VMEM((UNITS, rows, half), F32),
             pltpu.VMEM((UNITS, rows, half), BF16),
             pltpu.VMEM((UNITS, rows, half), BF16),
-            pltpu.VMEM((UNITS, 2, rows, half), BF16),
+            pltpu.VMEM((UNITS, rows, hidden), BF16),
             pltpu.VMEM((NZ, rows, features), F32),
             pltpu.VMEM((3, rows, features), BF16),
             pltpu.VMEM((NZ, rows, features), BF16),

time: 62.2 us -> 62.2 us (level)
  no operation moved by 1% of the time
where the time goes in v10:
time: 62.2 us; the launch traced here: 62 us
  Pallas kernels  60.3 us (97%)
  local copies, waits for them, and re-layouts  1.65 us (3%)
    pallas_call x1, Pallas kernels, dense(): pl.pallas_call(dense_kernel, out_shape=jax.ShapeDtypeStruct((rows, featur...  60.3 us
    unnamed x1, local copies, waits for them, and re-layouts  1.65 us

profile of v10, /device:TPU:0, one launch (start us, length us, event | category | flops | bytes accessed | tf_op | source)
XLA Modules:
  0.0 62.0 jit_solution(8153246758146564117)
XLA Ops:
  0.0 60.3 %shard_map.55 = bf16[128,896]{1,0:T(8,128)(2,1)} custom-call(bf16[128,896]{1,0:T(8,128)(2,1)} %tokens.1, s32[8,128]{1,0:T(8,128)} %bitcast.2, f32[8,128]{1,0:T(8,128)} %bitcast.3, bf16[1,896,1024]{2,1,0:T(8,128)(2,1)} %up.1, bf16[1,1024,896]{2,1,0:T(8,128)(2,1)} %down.1), custom_call_target="tpu_custom_call" | custom-call | flops 3758096384 | bytes 4128768 | tf_op jit(solution)/shard_map/pallas_call | solution.py:411
  60.3 1.6 %copy.7 = bf16[128,896]{1,0:T(8,128)(2,1)} copy(bf16[128,896]{1,0:T(8,128)(2,1)} %shard_map.55) | data formatting | bytes 458752

commit v11 on v10

--- a/solution.py
+++ b/solution.py
@@ -114,13 +114,13 @@
     own_x = token(0, tokens, 2, x_peer)
     own_near = token(1, tokens, 1, near)
     own_across = token(2, tokens, 3, across)
-    near_across = token(3, got.at[1], 5, across)
-    side_near = token(4, got.at[2], 6, near)
+    near_across = token(3, got.at[1], 6, across)
+    side_near = token(4, got.at[2], 5, near)
     across_near = token(5, got.at[3], 3, near)
-    far_near = token(6, got.at[5], 5, near)
+    far_near = token(6, got.at[6], 6, near)
     second_x = token(7, got.at[3], 4, x_peer)
-    third_x = token(8, got.at[5], 7, x_peer)
-    near_x = token(9, got.at[1], 6, x_peer)
+    third_x = token(8, got.at[6], 7, x_peer)
+    near_x = token(9, got.at[1], 5, x_peer)
 
     def weight(k):
         return remote(wt.at[0], wt.at[k], w_s.at[k], w_r.at[k], at(k // 2, k % 2 == 1))
@@ -217,10 +217,14 @@
                     side_near(0).start()
 
     def second_arrivals():
+        @pl.when(is_inner)
+        def _():
+            side_near(0).start()
+
         for p in range(2):
             @pl.when(is_inner)
             def _():
-                token_in(5, p).wait_recv()
+                token_in(6, p).wait_recv()
                 far_near(p).start()
                 third_x(p).start()
 
@@ -229,22 +233,15 @@
                 token_in(3, p).wait_recv()
                 second_x(p).start()
 
-        @pl.when(is_inner)
-        def _():
-            side_near(0).start()
-
     def third_arrivals():
         for p in range(2):
             @pl.when(jnp.logical_not(is_inner))
             def _():
-                token_in(5, p).wait_recv()
+                token_in(6, p).wait_recv()
                 third_x(p).start()
 
-        token_in(4, 0).wait_recv()
-        token_in(4, 1).wait_recv()
-
     def stage_a(u):
-        @pl.when(u >= 6)
+        @pl.when((u == 4) | (u == 5) | (u == 7))
         def _():
             token_in(u, 0).wait_recv()
             token_in(u, 1).wait_recv()
@@ -268,8 +265,8 @@
         hid_copy(u).start()
 
     def stage_d(u):
-        other = (u == 2) | (u == 4) | (u >= 6)
-        d = jnp.where((u == 1) | (u == 6), 1, jnp.where((u == 3) | (u == 4), second, third))
+        other = (u == 2) | (u == 4) | (u == 5) | (u == 7)
+        d = jnp.where((u == 1) | (u == 5), 1, jnp.where((u == 3) | (u == 4), second, third))
         d = jnp.where((u == 0) | (u == 2), 0, d)
         k = 2 * d + other.astype(jnp.int32)
 
@@ -282,7 +279,7 @@
         result = jnp.dot(hid[u], downv[...], preferred_element_type=F32)
         result = result * jnp.concatenate([scale] * (result.shape[1] // 128), axis=1)
 
-        @pl.when((u == 0) | (u == 3) | (u == 5))
+        @pl.when((u == 0) | (u == 3) | (u == 6))
         def _():
             acc[d] = result
 
@@ -299,7 +296,7 @@
         def _():
             over[0] = result.astype(BF16)
 
-        @pl.when(u == 6)
+        @pl.when(u == 5)
         def _():
             over[1] = result.astype(BF16)
             over_copy(0).start()
@@ -321,7 +318,7 @@
         def _():
             second_arrivals()
 
-        @pl.when(t == 4)
+        @pl.when(t == 5)
         def _():
             third_arrivals()
 
@@ -336,6 +333,14 @@
         @pl.when((t >= 2) & (t < UNITS + 2))
         def _():
             stage_c(t - 2)
+
+        @pl.when(t == UNITS + 2)
+        def _():
+            for p in range(2):
+                over_copy(p).wait_recv()
+                both = over[0, lines(p)].astype(F32) + over[2, lines(p)].astype(F32)
+                x_out[0, lines(p)] = both.astype(BF16)
+                x_copy(0, p).start()
 
         @pl.when((t >= 3) & (t < UNITS + 3))
         def _():
@@ -379,9 +384,6 @@
 
     for p in range(2):
         stage_e(third, p)
-        over_copy(p).wait_recv()
-        x_out[0, lines(p)] = (over[0, lines(p)].astype(F32) + over[2, lines(p)].astype(F32)).astype(BF16)
-        x_copy(0, p).start()
 
     for p in range(2):
         over_copy(p).wait_send()

time: 62.2 us -> 63.2 us (1.016)
  Pallas kernels: 60.3 us -> 61.3 us
    pallas_call x1, Pallas kernels: 60.3 us -> 61.3 us  [dense(): pl.pallas_call(dense_kernel, out_shape=jax.ShapeDtypeStruct((rows, featur...]
where the time goes in v11:
time: 63.2 us; the launch traced here: 63 us
  Pallas kernels  61.3 us (97%)
  local copies, waits for them, and re-layouts  1.65 us (3%)
    pallas_call x1, Pallas kernels, dense(): pl.pallas_call(dense_kernel, out_shape=jax.ShapeDtypeStruct((rows, featur...  61.3 us
    unnamed x1, local copies, waits for them, and re-layouts  1.65 us

profile of v11, /device:TPU:0, one launch (start us, length us, event | category | flops | bytes accessed | tf_op | source)
XLA Modules:
  0.0 63.0 jit_solution(9789205038193010455)
XLA Ops:
  0.0 61.3 %shard_map.55 = bf16[128,896]{1,0:T(8,128)(2,1)} custom-call(bf16[128,896]{1,0:T(8,128)(2,1)} %tokens.1, s32[8,128]{1,0:T(8,128)} %bitcast.2, f32[8,128]{1,0:T(8,128)} %bitcast.3, bf16[1,896,1024]{2,1,0:T(8,128)(2,1)} %up.1, bf16[1,1024,896]{2,1,0:T(8,128)(2,1)} %down.1), custom_call_target="tpu_custom_call" | custom-call | flops 3758096384 | bytes 4128768 | tf_op jit(solution)/shard_map/pallas_call | solution.py:413
  61.3 1.6 %copy.7 = bf16[128,896]{1,0:T(8,128)(2,1)} copy(bf16[128,896]{1,0:T(8,128)(2,1)} %shard_map.55) | data formatting | bytes 458752

commit v12 on v10

--- a/solution.py
+++ b/solution.py
@@ -131,8 +131,8 @@
     def core_copy(u):
         return remote(core_out.at[u], core_in.at[u], core_s.at[u], core_r.at[u], core_peer)
 
-    def y_copy(u):
-        return remote(y_out.at[u], y_in.at[u], y_s.at[u], y_r.at[u], y_peer)
+    def y_copy(u, p):
+        return remote(y_out.at[u, lines(p)], y_in.at[u, lines(p)], y_s.at[u, p], y_r.at[u, p], y_peer)
 
     def hid_copy(u):
         return remote(hid.at[u, :, :half], hid.at[u, :, half:], hid_s.at[u], hid_r.at[u], core_peer)
@@ -256,15 +256,17 @@
 
     def stage_b(u):
         core_copy(u).wait_recv()
-        total = kept[u] + core_in[u].astype(F32)
-        kept[u] = total
-        y_out[u] = total.astype(BF16)
-        y_copy(u).start()
+        for p in range(2):
+            total = kept[u, lines(p)] + core_in[u, lines(p)].astype(F32)
+            kept[u, lines(p)] = total
+            y_out[u, lines(p)] = total.astype(BF16)
+            y_copy(u, p).start()
 
     def stage_c(u):
-        y_copy(u).wait_recv()
-        before = kept[u] + y_in[u].astype(F32)
-        hid[u, :, :half] = (before / (1.0 + jnp.exp(-before))).astype(BF16)
+        for p in range(2):
+            y_copy(u, p).wait_recv()
+            before = kept[u, lines(p)] + y_in[u, lines(p)].astype(F32)
+            hid[u, lines(p), :half] = (before / (1.0 + jnp.exp(-before))).astype(BF16)
         hid_copy(u).start()
 
     def stage_d(u):
@@ -374,7 +376,8 @@
         if u:
             weight(u).wait_send()
         core_copy(u).wait_send()
-        y_copy(u).wait_send()
+        y_copy(u, 0).wait_send()
+        y_copy(u, 1).wait_send()
         hid_copy(u).wait_send()
 
     for p in range(2):
@@ -430,7 +433,7 @@
             pltpu.VMEM((NZ, rows, features), BF16),
             pltpu.VMEM((NZ, rows, features), BF16),
             pltpu.VMEM((NZ, rows, features), BF16),
-        ] + [dma((10, 2)), dma((UNITS, 2))] + [dma((UNITS,))] * 8 + [dma((NZ, 2))] * 4 + [dma((5,))],
+        ] + [dma((10, 2)), dma((UNITS, 2))] + [dma((UNITS,))] * 4 + [dma((UNITS, 2))] * 2 + [dma((UNITS,))] * 2 + [dma((NZ, 2))] * 4 + [dma((5,))],
         compiler_params=pltpu.CompilerParams(
             collective_id=0, has_side_effects=True, vmem_limit_bytes=63 * 2**20
         ),

time: 62.2 us -> 62.3 us (level)
  no operation moved by 1% of the time
where the time goes in v12:
time: 62.3 us; the launch traced here: 62.1 us
  Pallas kernels  60.4 us (97%)
  local copies, waits for them, and re-layouts  1.65 us (3%)
    pallas_call x1, Pallas kernels, dense(): pl.pallas_call(dense_kernel, out_shape=jax.ShapeDtypeStruct((rows, featur...  60.4 us
    unnamed x1, local copies, waits for them, and re-layouts  1.65 us

profile of v12, /device:TPU:0, one launch (start us, length us, event | category | flops | bytes accessed | tf_op | source)
XLA Modules:
  0.0 62.1 jit_solution(6315695894861555356)
XLA Ops:
  0.0 60.4 %shard_map.55 = bf16[128,896]{1,0:T(8,128)(2,1)} custom-call(bf16[128,896]{1,0:T(8,128)(2,1)} %tokens.1, s32[8,128]{1,0:T(8,128)} %bitcast.2, f32[8,128]{1,0:T(8,128)} %bitcast.3, bf16[1,896,1024]{2,1,0:T(8,128)(2,1)} %up.1, bf16[1,1024,896]{2,1,0:T(8,128)(2,1)} %down.1), custom_call_target="tpu_custom_call" | custom-call | flops 3758096384 | bytes 4128768 | tf_op jit(solution)/shard_map/pallas_call | solution.py:414
  60.4 1.6 %copy.7 = bf16[128,896]{1,0:T(8,128)(2,1)} copy(bf16[128,896]{1,0:T(8,128)(2,1)} %shard_map.55) | data formatting | bytes 458752
